TPU v7x, 256 devices: a whole 4x4x8 slice. The times are simulated.
256 devices in a mesh: seq: 64 (over z_hi, y, x), red: 4 (over z_lo, core).
Axes of the slice: x: 4, y: 4, z: 8 (z_hi: 4, z_lo: 2; z = z_hi * 2 + z_lo), core: 2. Of those that a mesh axis runs over, the one named last changes fastest.
Arguments:
- token_ids: int32 [8192], P('seq'), may hold values from 0 to 511
- embedding: bfloat16 [512, 4096], P(None, 'red'), may hold values from -6 to 6
- proj_weight: bfloat16 [4096, 3, 4, 256], P('red', None, None, 'seq'), may hold values from -0.09375 to 0.09375
- filters: float32 [8192, 1024], P('seq', 'red'), may hold values from -1 to 1
- cotangent: float32 [8192, 1024], P('seq', 'red'), may hold values from -6 to 6
Outputs:
- output: float32 [8192, 1024], P('seq', 'red')
- filter_grad: float32 [8192, 1024], P('seq', 'red')
- branch_grads: bfloat16 [8192, 3, 1024], P('seq', None, 'red')
- weight_grad: float32 [4096, 3, 4, 256], P('red', None, None, 'seq')
All inputs are finite; a program needn't handle non-finite values.
Results may differ from a plain program's by a relative error of at most 0.0029.
Values sent between devices are 32-bit elements; how exact they have to be, the bound alone decides.
No kernel may reach another device: no remote copies, remote signals or barrier semaphores. Data moves between devices by JAX's collectives and lax.ppermute only.
A program may use at most 64 MiB of HBM per device.

v0:
```python
import math

import jax
import jax.numpy as jnp
from jax import lax
from jax.sharding import PartitionSpec as P

precise_mode = lax.Precision.HIGHEST


def in_blocks(value, dim, length):
    before, after = (value.shape[:dim], value.shape[dim + 1 :])
    return jnp.moveaxis(value.reshape(*before, length, -1, *after), dim, 0)


def summed_on_arrival(value, axis, dim):
    tiles = in_blocks(value, dim, lax.axis_size(axis))
    arrived = lax.all_to_all(tiles, axis, split_axis=0, concat_axis=0, tiled=True)
    return arrived.sum(axis=0)


def copy_for_each(value, axis):
    length = lax.axis_size(axis)
    return lax.all_to_all(
        jnp.broadcast_to(value[None], (length, *value.shape)), axis, 0, 0, tiled=True
    )


def in_order(tiles, dim):
    tiles = jnp.moveaxis(tiles, 0, dim)
    shape = tiles.shape
    return tiles.reshape(*shape[:dim], shape[dim] * shape[dim + 1], *shape[dim + 2 :])


def gather_directly(value, axis, dim):
    tiles = copy_for_each(value, axis)
    return in_order(tiles, dim)


def angles(numbers, modulus, direction):
    phase = (numbers % modulus).astype(jnp.float32) * (direction * 2.0 * math.pi / modulus)
    return (jnp.cos(phase), jnp.sin(phase))


def rotate(real_part, imag_part, cosine, sine_part):
    return (real_part * cosine - imag_part * sine_part, real_part * sine_part + imag_part * cosine)


def complex_einsum(formula, matrix, values):
    mat_real, mat_imag = matrix
    val_real, val_imag = values
    real_out = jnp.einsum(formula, mat_real, val_real, precision=precise_mode) - jnp.einsum(
        formula, mat_imag, val_imag, precision=precise_mode
    )
    imag_out = jnp.einsum(formula, mat_real, val_imag, precision=precise_mode) + jnp.einsum(
        formula, mat_imag, val_real, precision=precise_mode
    )
    return (real_out, imag_out)


def factors(length_total):
    first_factor = 1
    for candidate in range(1, math.isqrt(length_total) + 1):
        if length_total % candidate == 0:
            first_factor = candidate
    return (first_factor, length_total // first_factor)


def combine_spectra(spec_real, spec_imag, width):
    filt_re = spec_real[..., :width]
    inner_re = spec_real[..., width : 2 * width]
    up_re = spec_real[..., 2 * width :]
    filt_im = spec_imag[..., :width]
    inner_im = spec_imag[..., width : 2 * width]
    up_im = spec_imag[..., 2 * width :]
    joined_real = jnp.concatenate(
        [
            filt_re * inner_re - filt_im * inner_im,
            filt_re * up_re + filt_im * up_im,
            up_re * inner_re + up_im * inner_im,
        ],
        axis=-1,
    )
    joined_imag = jnp.concatenate(
        [
            filt_re * inner_im + filt_im * inner_re,
            filt_re * up_im - filt_im * up_re,
            up_im * inner_re - up_re * inner_im,
        ],
        axis=-1,
    )
    return (joined_real, joined_imag)


def local_convolve(signals):
    length, branch_count, narrow = signals.shape
    total = 2 * length
    first_factor, second_factor = factors(total)
    flat = signals.reshape(length, branch_count * narrow)
    padded = jnp.concatenate([flat, jnp.zeros_like(flat)], axis=0).reshape(
        first_factor, second_factor, branch_count * narrow
    )
    first_index = jnp.arange(first_factor, dtype=jnp.int32)
    second_index = jnp.arange(second_factor, dtype=jnp.int32)
    cosine, sine_part = angles(first_index[:, None] * first_index[None, :], first_factor, -1.0)
    real_part = jnp.einsum("kn,nbm->kbm", cosine, padded, precision=precise_mode)
    imag_part = jnp.einsum("kn,nbm->kbm", sine_part, padded, precision=precise_mode)
    cosine, sine_part = angles(first_index[:, None] * second_index[None, :], total, -1.0)
    real_part, imag_part = rotate(real_part, imag_part, cosine[:, :, None], sine_part[:, :, None])
    real_part, imag_part = complex_einsum(
        "lb,kbm->klm",
        angles(second_index[:, None] * second_index[None, :], second_factor, -1.0),
        (real_part, imag_part),
    )
    real_part, imag_part = combine_spectra(real_part, imag_part, narrow)
    real_part, imag_part = complex_einsum(
        "bl,klm->kbm",
        angles(second_index[:, None] * second_index[None, :], second_factor, 1.0),
        (real_part, imag_part),
    )
    cosine, sine_part = angles(first_index[:, None] * second_index[None, :], total, 1.0)
    real_part, imag_part = rotate(real_part, imag_part, cosine[:, :, None], sine_part[:, :, None])
    cosine, sine_part = angles(first_index[:, None] * first_index[None, :], first_factor, 1.0)
    result = jnp.einsum("nk,kbm->nbm", cosine, real_part, precision=precise_mode) - jnp.einsum(
        "nk,kbm->nbm", sine_part, imag_part, precision=precise_mode
    )
    result = result.reshape(total, branch_count * narrow)[:length] / total
    return result.reshape(length, branch_count, narrow)


def shards(token_ids, embedding, proj_weight, filters, cotangent):
    tok_count = token_ids.shape[0]
    devices = lax.axis_size("seq")
    width = filters.shape[1]
    vocabulary = embedding.shape[0]
    width_rows, branches, red_count, piece = proj_weight.shape
    scale_factor = float(tok_count * devices) ** (-0.5)
    table = jnp.dot(
        embedding,
        proj_weight.reshape(width_rows, branches * red_count * piece),
        preferred_element_type=jnp.float32,
    )
    table = table.reshape(vocabulary, branches, red_count, piece)
    own_table = summed_on_arrival(table, "red", 2)
    full_table = gather_directly(own_table, "seq", 3)
    projected = jnp.take(full_table, token_ids, axis=0)
    projected = projected.reshape(tok_count, branches, width)
    queries = projected[:, 0]
    key_rows = projected[:, 1]
    value_rows = projected[:, 2]
    inner = key_rows * value_rows
    upstream = cotangent * queries
    stacked = jnp.stack([filters, inner, upstream], axis=1)
    whole_length = lax.all_to_all(stacked, "seq", split_axis=2, concat_axis=0, tiled=True)
    results = local_convolve(whole_length)
    returned = lax.all_to_all(results, "seq", split_axis=0, concat_axis=2, tiled=True)
    conv = returned[:, 0]
    grad_inner = returned[:, 1]
    filter_raw = returned[:, 2]
    output = queries * conv
    filter_grad = filter_raw * scale_factor
    branch_grads = jnp.stack(
        [cotangent * conv, grad_inner * value_rows, grad_inner * key_rows], axis=1
    ).astype(jnp.bfloat16)
    one_hot = (token_ids[:, None] == lax.iota(jnp.int32, vocabulary)[None, :]).astype(jnp.bfloat16)
    token_sums = lax.dot_general(
        one_hot,
        branch_grads.reshape(tok_count, branches * width),
        (((0,), (0,)), ((), ())),
        preferred_element_type=jnp.float32,
    )
    summed = summed_on_arrival(token_sums.reshape(vocabulary, branches, width), "seq", 2)
    gathered = gather_directly(summed[:, :, None, :], "red", 2)
    weight_grad = (
        lax.dot_general(
            embedding.astype(jnp.float32),
            gathered.reshape(vocabulary, branches * red_count * piece),
            (((0,), (0,)), ((), ())),
            precision=precise_mode,
        )
        * scale_factor
    )
    return (
        output,
        filter_grad,
        branch_grads,
        weight_grad.reshape(width_rows, branches, red_count, piece),
    )


def solution(mesh):
    in_specs = (
        P("seq"),
        P(None, "red"),
        P("red", None, None, "seq"),
        P("seq", "red"),
        P("seq", "red"),
    )
    out_specs = (
        P("seq", "red"),
        P("seq", "red"),
        P("seq", None, "red"),
        P("red", None, None, "seq"),
    )
    return jax.shard_map(shards, mesh=mesh, in_specs=in_specs, out_specs=out_specs, check_vma=False)
```

profile of v0, /device:TPU:32, one launch (start us, length us, event | category | flops | bytes accessed | tf_op | source)
XLA Modules:
  0.0 238.8 jit_solution(10747169346815855003)
XLA Ops:
  0.6 1.0 reshape.117
  1.9 0.5 convolution_bitcast_fusion.1
  2.4 6.8 %all_to_all.53 = f32[4,512,3,1,4]{1,4,2,3,0:T(4,128)S(1)} all-to-all(f32[4,512,3,1,4]{1,4,2,3,0:T(4,128)S(1)} %copy.50), channel_id=1, replica_groups=mesh['seq'=64,'red'=4] {'red'}, dimensions={0} | all-to-all | bytes 196608 | tf_op jit(solution)/shard_map/all_to_all | solution.py:18
  9.2 1.4 broadcast_in_dim.17
  10.6 13.0 %all-to-all-start.1 = ((f32[64,512,3,1,4]{1,4,2,3,0:T(4,128)}), f32[64,512,3,1,4]{1,4,2,3,0:T(4,128)S(1)}, u32[]{:S(2)}, u32[]{:S(2)}) async-start(f32[64,512,3,1,4]{1,4,2,3,0:T(4,128)} %broadcast_in_dim.17), calls=%async_computation.1 | async-start | bytes 3145728 | tf_op jit(solution)/shard_map/all_to_all | solution.py:24
  23.7 35.9 %all-to-all-done.1 = f32[64,512,3,1,4]{1,4,2,3,0:T(4,128)S(1)} async-done(((f32[64,512,3,1,4]{1,4,2,3,0:T(4,128)}), f32[64,512,3,1,4]{1,4,2,3,0:T(4,128)S(1)}, u32[]{:S(2)}, u32[]{:S(2)}) %all-to-all-start.1) | async-done | bytes 1572896 | tf_op jit(solution)/shard_map/all_to_all | solution.py:24
  59.6 1.5 copy.51
  61.1 1.8 reshape.123
  63.0 1.8 copy.52
  64.8 2.5 %gather_fusion = f32[128,3,256]{2,1,0:T(4,128)S(1)} fusion(f32[512,3,256]{2,1,0:T(4,128)} %copy.52, s32[1024]{0:T(1024)S(1)} %pad_clamp_fusion), kind=kCustom, calls=%fused_computation | custom fusion | bytes 786944 | tf_op jit(solution)/shard_map/jit(_take)/gather | solution.py:146
  67.9 0.3 pad_maximum_fusion.6
  68.3 1.0 copy.54
  69.3 11.8 %all-to-all-start.2 = ((f32[128,3,256]{0,1,2:T(4,128)}), f32[128,3,256]{0,1,2:T(4,128)S(1)}, u32[]{:S(2)}, u32[]{:S(2)}) async-start(f32[128,3,256]{0,1,2:T(4,128)} %copy.54), calls=%async_computation.2 | async-start | bytes 1048576 | tf_op jit(solution)/shard_map/all_to_all | solution.py:154
  81.6 18.6 %all-to-all-done.2 = f32[128,3,256]{0,1,2:T(4,128)S(1)} async-done(((f32[128,3,256]{0,1,2:T(4,128)}), f32[128,3,256]{0,1,2:T(4,128)S(1)}, u32[]{:S(2)}, u32[]{:S(2)}) %all-to-all-start.2) | async-done | bytes 393248 | tf_op jit(solution)/shard_map/all_to_all | solution.py:154
  100.4 0.3 copy.73
  101.0 1.1 fusion.4
  102.0 1.1 fusion.6
  103.1 1.0 fusion.30
  104.1 1.0 fusion.31
  105.2 1.0 fusion.1
  106.2 1.0 fusion
  107.5 1.0 fusion.21
  108.5 1.0 fusion.20
  109.5 1.0 convolution_subtract_fusion
  110.5 1.0 convolution_add_fusion
  111.6 1.3 fusion.10
  112.9 1.1 fusion.8
  114.2 10.7 %copy.57 = f32[8192,3,4]{2,1,0:T(4,128)} copy(f32[8192,3,4]{0,2,1:T(4,128)S(1)} %div.10) | data formatting | bytes 786432 | tf_op jit(solution)/shard_map/div | solution.py:127
  124.9 16.0 %reshape.142 = f32[64,1,1536]{2,1,0:T(1,128)S(1)} reshape(f32[8192,3,4]{2,1,0:T(4,128)} %copy.57) | data formatting | bytes 786432
  140.9 20.0 %all_to_all.54 = f32[64,1,1536]{2,1,0:T(1,128)S(1)} all-to-all(f32[64,1,1536]{2,1,0:T(1,128)S(1)} %reshape.142), channel_id=1, replica_groups=mesh['seq'=64,'red'=4] {'seq'}, dimensions={0} | all-to-all | bytes 786432 | tf_op jit(solution)/shard_map/all_to_all | solution.py:156
  160.9 0.5 broadcast.243
  161.4 1.6 reduce.1
  163.0 11.5 %reshape.143 = f32[8192,3,4]{2,1,0:T(4,128)} reshape(f32[64,1536]{1,0:T(8,128)S(1)} %reduce.1) | data formatting | bytes 786432
  174.5 11.7 %copy.58 = f32[64,128,3,4]{1,3,0,2:T(4,128)S(1)} copy(f32[64,128,3,4]{3,2,1,0:T(4,128)} %bitcast.114) | data formatting | bytes 786432 | tf_op jit(solution)/shard_map/all_to_all | solution.py:156
  186.4 0.3 slice_multiply_fusion.1
  187.0 0.5 maximum_convert_fusion
  187.7 0.5 convolution_bitcast_fusion
  188.1 2.2 copy.64
  190.3 5.4 %all-to-all-start.4 = ((f32[64,512,3,4]{1,3,2,0:T(4,128)}), f32[64,512,3,4]{1,3,2,0:T(4,128)S(1)}, u32[]{:S(2)}, u32[]{:S(2)}) async-start(f32[64,512,3,4]{1,3,2,0:T(4,128)} %copy.64), calls=%async_computation.4 | async-start | bytes 3145728 | tf_op jit(solution)/shard_map/all_to_all | solution.py:18
  195.7 0.7 copy.67
  196.4 0.8 copy.66
  197.1 33.4 %all-to-all-done.4 = f32[64,512,3,4]{1,3,2,0:T(4,128)S(1)} async-done(((f32[64,512,3,4]{1,3,2,0:T(4,128)}), f32[64,512,3,4]{1,3,2,0:T(4,128)S(1)}, u32[]{:S(2)}, u32[]{:S(2)}) %all-to-all-start.4) | async-done | bytes 1572896 | tf_op jit(solution)/shard_map/all_to_all | solution.py:18
  230.8 0.7 broadcast_in_dim.20
  231.4 3.3 %all-to-all-start.5 = ((f32[4,512,3,1,4]{1,4,2,3,0:T(4,128)}), f32[4,512,3,1,4]{1,4,2,3,0:T(4,128)S(1)}, u32[]{:S(2)}, u32[]{:S(2)}) async-start(f32[4,512,3,1,4]{1,4,2,3,0:T(4,128)} %broadcast_in_dim.20), calls=%async_computation.5 | async-start | bytes 196608 | tf_op jit(solution)/shard_map/all_to_all | solution.py:24
  234.7 0.7 bitcast_multiply_fusion.1
  235.4 1.9 all-to-all-done.5
  237.4 0.6 fusion.2
  238.0 0.7 reshape.122
  (39 shorter events, 3.2 us)
Async XLA Ops:
  0.6 1.3 copy-start
  10.6 13.0 %copy-start.2 = (f32[128,256]{1,0:T(8,128)S(1)}, f32[128,256]{1,0:T(8,128)}, u32[]{:S(2)}) copy-start(f32[128,256]{1,0:T(8,128)} %param.8) | copy-start | bytes 393220
  10.6 13.1 %copy-start.3 = (s32[128]{0:T(128)S(1)}, s32[128]{0:T(128)}, u32[]{:S(2)}) copy-start(s32[128]{0:T(128)} %param.5) | copy-start | bytes 1540
  10.6 49.0 %all-to-all-start.1 = ((f32[64,512,3,1,4]{1,4,2,3,0:T(4,128)}), f32[64,512,3,1,4]{1,4,2,3,0:T(4,128)S(1)}, u32[]{:S(2)}, u32[]{:S(2)}) async-start(f32[64,512,3,1,4]{1,4,2,3,0:T(4,128)} %broadcast_in_dim.17), calls=%async_computation.1 | async-start | bytes 3145728 | tf_op jit(solution)/shard_map/all_to_all | solution.py:24
  64.8 3.0 %copy-start.1 = (f32[128,256]{1,0:T(8,128)S(1)}, f32[128,256]{1,0:T(8,128)}, u32[]{:S(2)}) copy-start(f32[128,256]{1,0:T(8,128)} %param.9) | copy-start | bytes 393220
  69.3 30.9 %all-to-all-start.2 = ((f32[128,3,256]{0,1,2:T(4,128)}), f32[128,3,256]{0,1,2:T(4,128)S(1)}, u32[]{:S(2)}, u32[]{:S(2)}) async-start(f32[128,3,256]{0,1,2:T(4,128)} %copy.54), calls=%async_computation.2 | async-start | bytes 1048576 | tf_op jit(solution)/shard_map/all_to_all | solution.py:154
  190.3 40.2 %all-to-all-start.4 = ((f32[64,512,3,4]{1,3,2,0:T(4,128)}), f32[64,512,3,4]{1,3,2,0:T(4,128)S(1)}, u32[]{:S(2)}, u32[]{:S(2)}) async-start(f32[64,512,3,4]{1,3,2,0:T(4,128)} %copy.64), calls=%async_computation.4 | async-start | bytes 3145728 | tf_op jit(solution)/shard_map/all_to_all | solution.py:18
  231.4 5.9 %all-to-all-start.5 = ((f32[4,512,3,1,4]{1,4,2,3,0:T(4,128)}), f32[4,512,3,1,4]{1,4,2,3,0:T(4,128)S(1)}, u32[]{:S(2)}, u32[]{:S(2)}) async-start(f32[4,512,3,1,4]{1,4,2,3,0:T(4,128)} %broadcast_in_dim.20), calls=%async_computation.5 | async-start | bytes 196608 | tf_op jit(solution)/shard_map/all_to_all | solution.py:24
where the time goes:
time: 242 us; the launch traced here: 239 us
  waiting for transfers between devices  89.8 us (37%)
  local copies, waits for them, and re-layouts  68.4 us (28%)
  starting transfers between devices  33.4 us (14%)
  blocking collectives  26.8 us (11%)
  matrix products  14.3 us (6%)
  other arithmetic  4.98 us (2%)
    all_to_all x2, waiting for transfers between devices, copy_for_each(): lax.all_to_all(jnp.broadcast_to(value[None], (length, *value.shape)), axi...  37.8 us
    all_to_all x1, waiting for transfers between devices, summed_on_arrival(): lax.all_to_all(tiles, axis, split_axis=0, concat_axis=0, tiled=True)  33.4 us
    unnamed x17, local copies, waits for them, and re-layouts  30 us
    all_to_all x1, blocking collectives, shards(): lax.all_to_all(results, 'seq', split_axis=0, concat_axis=2, tiled=True)  20 us
    all_to_all x1, waiting for transfers between devices, shards(): lax.all_to_all(stacked, 'seq', split_axis=2, concat_axis=0, tiled=True)  18.6 us
    all_to_all x2, starting transfers between devices, copy_for_each(): lax.all_to_all(jnp.broadcast_to(value[None], (length, *value.shape)), axi...  16.3 us
    all_to_all x2, local copies, waits for them, and re-layouts, shards(): lax.all_to_all(results, 'seq', split_axis=0, concat_axis=2, tiled=True)  12.2 us
    all_to_all x1, starting transfers between devices, shards(): lax.all_to_all(stacked, 'seq', split_axis=2, concat_axis=0, tiled=True)  11.8 us
  transfers between devices with their start and end apart: 4, of which 4 were waited for; matrix products, arithmetic and copies ran while one was open for 1% of the time, Pallas kernels for 0%

commit v1 on v0

v1 whole, which is shorter than its diff:
```python
import functools
import math

import jax
import jax.numpy as jnp
import ml_dtypes
import numpy as np
from jax import lax
from jax.experimental import pallas as pl
from jax.experimental.pallas import tpu as pltpu
from jax.sharding import PartitionSpec as P


BLOCKS = 64
LANES = 128
OWN = 4
IN_ROWS = 9
OUT_ROWS = 20
F32 = jnp.float32
BF16 = jnp.bfloat16


def halves(matrix):
    matrix = np.asarray(matrix, np.float32)
    high = matrix.astype(ml_dtypes.bfloat16)
    low = (matrix - high.astype(np.float32)).astype(ml_dtypes.bfloat16)
    return high, low


@functools.cache
def transform_constants():
    odd = np.arange(BLOCKS) + 0.5
    theta = 2.0 * math.pi * np.outer(odd, np.arange(BLOCKS)) / LANES
    rows = np.concatenate([np.cos(theta), -np.sin(theta)], axis=0)
    high, low = halves(rows)
    first = np.concatenate([high, high, low], axis=1)
    high, low = halves(rows.T * (2.0 / (2 * BLOCKS * LANES)))
    last = np.concatenate([high, high, low], axis=1)
    phi = 2.0 * math.pi * np.outer(odd, np.arange(LANES)) / (2 * BLOCKS * LANES)
    twiddle = np.stack([np.cos(phi), np.sin(phi)]).astype(np.float32)
    psi = 2.0 * math.pi * (np.outer(np.arange(LANES), np.arange(LANES)) % LANES) / LANES
    right = np.block([[np.cos(psi), -np.sin(psi)], [np.sin(psi), np.cos(psi)]])
    forward = np.stack(halves(right))
    backward = np.stack(halves(right.T))
    return first, last, twiddle, forward, backward


def split(value):
    high = value.astype(BF16)
    return high, (value - high.astype(F32)).astype(BF16)


def dot(left, right):
    return jnp.dot(left, right, preferred_element_type=F32)


def dot_last(left, right):
    return lax.dot_general(left, right, (((1,), (1,)), ((), ())), preferred_element_type=F32)


def pack_kernel(ids_ref, filt_ref, cot_ref, out_ref, turn_ref):
    for number, ref in enumerate((filt_ref, cot_ref)):
        turn_ref[...] = ref[...].T
        for c in range(OWN):
            out_ref[pl.ds(number * OWN + c, BLOCKS, stride=IN_ROWS), :] = turn_ref[
                pl.ds(c, BLOCKS, stride=OWN), :
            ]
    out_ref[pl.ds(2 * OWN, BLOCKS, stride=IN_ROWS), :] = jnp.broadcast_to(
        ids_ref[...].astype(F32), (BLOCKS, LANES)
    )


def table_kernel(proj_ref, emb_ref, out_ref, rows_ref):
    branches, reds, piece, _ = proj_ref.shape
    wide = branches * piece
    for q in range(reds):
        for b in range(branches):
            at = q * wide + b * piece
            rows_ref[at : at + piece, :] = proj_ref[b, q].astype(F32)
    table = dot_last(rows_ref[...].astype(BF16), emb_ref[...])
    for q in range(reds):
        for part in range(table.shape[1] // LANES):
            out_ref[q, part * wide : (part + 1) * wide, :] = table[
                q * wide : (q + 1) * wide, part * LANES : (part + 1) * LANES
            ]


def right_product(value, matrix_ref):
    high, low = split(value)
    count = value.shape[0]
    both = dot(jnp.concatenate([high, low], axis=0), matrix_ref[0])
    return both[:count] + both[count:] + dot(high, matrix_ref[1])


def conv_kernel(
    scale, in_ref, parts_ref, first_ref, last_ref, twiddle_ref, forward_ref, backward_ref, out_ref, grads_ref
):
    reds, table_rows, _ = parts_ref.shape
    wide = 3 * OWN
    groups = table_rows // wide

    def received(row):
        return in_ref[pl.ds(row, BLOCKS, stride=IN_ROWS), :]

    table = parts_ref[0]
    for q in range(1, reds):
        table = table + parts_ref[q]
    ids = received(2 * OWN).astype(jnp.int32)
    lane = ids & (LANES - 1)
    group = ids >> 7

    def looked_up(column):
        value = None
        for g in range(groups):
            row = jnp.broadcast_to(table[g * wide + column : g * wide + column + 1, :], (BLOCKS, LANES))
            found = jnp.take_along_axis(row, lane, axis=1, mode="promise_in_bounds")
            value = found if value is None else jnp.where(group == g, found, value)
        return value

    queries = [looked_up(c) for c in range(OWN)]
    keys = [looked_up(OWN + c) for c in range(OWN)]
    values = [looked_up(2 * OWN + c) for c in range(OWN)]
    cotangent = [received(OWN + c) for c in range(OWN)]
    signals = [received(c) for c in range(OWN)]
    signals += [keys[c] * values[c] for c in range(OWN)]
    signals += [cotangent[c] * queries[c] for c in range(OWN)]
    count = len(signals)

    cosine, sine = twiddle_ref[0], twiddle_ref[1]
    high, low = split(jnp.concatenate(signals, axis=1))
    mixed = dot(first_ref[...], jnp.concatenate([high, low, high], axis=0))
    rows = []
    for n in range(count):
        re = mixed[:BLOCKS, n * LANES : (n + 1) * LANES]
        im = mixed[BLOCKS:, n * LANES : (n + 1) * LANES]
        rows.append(jnp.concatenate([re * cosine + im * sine, im * cosine - re * sine], axis=1))
    spectra = right_product(jnp.concatenate(rows, axis=0), forward_ref)

    def spectrum(n):
        own = spectra[n * BLOCKS : (n + 1) * BLOCKS]
        return own[:, :LANES], own[:, LANES:]

    joined = [None] * count
    for c in range(OWN):
        f_re, f_im = spectrum(c)
        i_re, i_im = spectrum(OWN + c)
        u_re, u_im = spectrum(2 * OWN + c)
        joined[c] = (f_re * i_re - f_im * i_im, f_re * i_im + f_im * i_re)
        joined[OWN + c] = (f_re * u_re + f_im * u_im, f_re * u_im - f_im * u_re)
        joined[2 * OWN + c] = (u_re * i_re + u_im * i_im, u_im * i_re - u_re * i_im)
    back = right_product(
        jnp.concatenate([jnp.concatenate(pair, axis=1) for pair in joined], axis=0), backward_ref
    )
    columns = []
    for n in range(count):
        re = back[n * BLOCKS : (n + 1) * BLOCKS, :LANES]
        im = back[n * BLOCKS : (n + 1) * BLOCKS, LANES:]
        columns.append(jnp.concatenate([re * cosine - im * sine, re * sine + im * cosine], axis=0))
    high, low = split(jnp.concatenate(columns, axis=1))
    result = dot(last_ref[...], jnp.concatenate([high, low, high], axis=0))

    grads_ref[...] = jnp.zeros_like(grads_ref)
    for c in range(OWN):
        conv = result[:, c * LANES : (c + 1) * LANES]
        grad_inner = result[:, (OWN + c) * LANES : (OWN + c + 1) * LANES]
        filter_grad = result[:, (2 * OWN + c) * LANES : (2 * OWN + c + 1) * LANES]
        grads = (cotangent[c] * conv, grad_inner * values[c], grad_inner * keys[c])
        sent = (*grads, queries[c] * conv, filter_grad * scale)
        for number, value in enumerate(sent):
            out_ref[pl.ds(number * OWN + c, BLOCKS, stride=OUT_ROWS), :] = value
        for number, value in enumerate(grads):
            grads_ref[pl.ds(number * OWN + c, BLOCKS, stride=16), :] = value


def sums_kernel(in_ref, grads_ref, out_ref, ids_ref):
    ids_ref[...] = in_ref[pl.ds(2 * OWN, BLOCKS, stride=IN_ROWS), :].astype(jnp.int32)
    groups = out_ref.shape[0] // 16
    total = jnp.zeros(out_ref.shape, F32)
    for pair in range(BLOCKS // 2):
        picked, hot = [], []
        for s in (2 * pair, 2 * pair + 1):
            ids = ids_ref[s : s + 1, :]
            grads = grads_ref[s * 16 : (s + 1) * 16, :]
            group = jnp.broadcast_to(ids >> 7, (16, LANES))
            picked.append(
                jnp.concatenate([jnp.where(group == g, grads, 0.0) for g in range(groups)], axis=0).astype(BF16)
            )
            lane = jnp.broadcast_to(ids & (LANES - 1), (LANES, LANES))
            rows = lax.broadcasted_iota(jnp.int32, (LANES, LANES), 0)
            hot.append(jnp.where(rows == lane, 1.0, 0.0).astype(BF16))
        total = total + dot_last(jnp.concatenate(picked, axis=1), jnp.concatenate(hot, axis=1))
    out_ref[...] = total


def weight_kernel(scale, sums_ref, emb_ref, out_ref):
    branches, reds, piece, _ = out_ref.shape
    groups = sums_ref.shape[1] // 16
    rows = jnp.concatenate(
        [
            jnp.concatenate([sums_ref[q, g * 16 : (g + 1) * 16, :] for g in range(groups)], axis=1)
            for q in range(reds)
        ],
        axis=0,
    )
    high, low = split(rows)
    count = rows.shape[0]
    both = dot(jnp.concatenate([high, low], axis=0), emb_ref[...])
    grad = (both[:count] + both[count:]) * scale
    for q in range(reds):
        for b in range(branches):
            at = q * 16 + b * piece
            out_ref[b, q] = grad[at : at + piece, :]


def unpack_kernel(in_ref, output_ref, filter_ref, branch_ref, turn_ref):
    for number in range(OUT_ROWS // OWN):
        for c in range(OWN):
            turn_ref[number, pl.ds(c, BLOCKS, stride=OWN), :] = in_ref[
                pl.ds(number * OWN + c, BLOCKS, stride=OUT_ROWS), :
            ]
        value = turn_ref[number].T
        if number < 3:
            branch_ref[number] = value.astype(BF16)
        elif number == 3:
            output_ref[...] = value
        else:
            filter_ref[...] = value


def call(body, outs, scratch, *operands):
    single = not isinstance(outs, (list, tuple))
    return pl.pallas_call(
        body,
        out_shape=outs if single else tuple(outs),
        scratch_shapes=scratch,
        compiler_params=pltpu.CompilerParams(vmem_limit_bytes=48 * 2**20),
    )(*operands)


def shape(dims, dtype=F32):
    return jax.ShapeDtypeStruct(dims, dtype)


def exchange(value, axis, pieces, rows):
    sent = value.reshape(pieces, 1, rows * LANES)
    got = lax.all_to_all(sent, axis, split_axis=0, concat_axis=0, tiled=True)
    return got.reshape(pieces * rows, LANES)


def shards(token_ids, embedding, proj_weight, filters, cotangent):
    reds = lax.axis_size("red")
    blocks = lax.axis_size("seq")
    width_rows, branches, _, piece = proj_weight.shape
    vocabulary = embedding.shape[0]
    groups = vocabulary // LANES
    positions, channels = filters.shape
    scale = float(positions * blocks) ** (-0.5)

    packed = call(
        pack_kernel,
        shape((BLOCKS * IN_ROWS, LANES)),
        [pltpu.VMEM((channels, LANES), F32)],
        token_ids.reshape(1, positions),
        filters,
        cotangent,
    )
    arrived = exchange(packed, "seq", BLOCKS, IN_ROWS)
    table = call(
        table_kernel,
        shape((reds, groups * branches * piece, LANES)),
        [pltpu.VMEM((reds * branches * piece, width_rows), F32)],
        proj_weight.transpose(1, 2, 3, 0),
        embedding,
    )
    parts = lax.all_to_all(table, "red", split_axis=0, concat_axis=0, tiled=True)
    constants = [jnp.asarray(c) for c in transform_constants()]
    results, grads = call(
        functools.partial(conv_kernel, scale),
        [shape((BLOCKS * OUT_ROWS, LANES)), shape((BLOCKS * 16, LANES))],
        [],
        arrived,
        parts,
        *constants,
    )
    returned = exchange(results, "seq", BLOCKS, OUT_ROWS)
    sums = call(
        sums_kernel,
        shape((groups * 16, LANES)),
        [pltpu.VMEM((BLOCKS, LANES), jnp.int32)],
        arrived,
        grads,
    )
    gathered = lax.all_gather(sums, "red", axis=0)
    weight_grad = call(
        functools.partial(weight_kernel, scale),
        shape((branches, reds, piece, width_rows)),
        [],
        gathered,
        embedding,
    )
    output, filter_grad, branch_grads = call(
        unpack_kernel,
        [
            shape((positions, channels)),
            shape((positions, channels)),
            shape((branches, positions, channels), BF16),
        ],
        [pltpu.VMEM((OUT_ROWS // OWN, channels, LANES), F32)],
        returned,
    )
    return output, filter_grad, branch_grads.transpose(1, 0, 2), weight_grad.transpose(3, 0, 1, 2)


def solution(mesh):
    in_specs = (
        P("seq"),
        P(None, "red"),
        P("red", None, None, "seq"),
        P("seq", "red"),
        P("seq", "red"),
    )
    out_specs = (
        P("seq", "red"),
        P("seq", "red"),
        P("seq", None, "red"),
        P("red", None, None, "seq"),
    )
    return jax.shard_map(shards, mesh=mesh, in_specs=in_specs, out_specs=out_specs, check_vma=False)
```

time: 242 us -> 73.2 us (0.30)
  the two profiles are of different devices: /device:TPU:32 before, /device:TPU:1 now
where the time goes in v1:
time: 73.2 us; the launch traced here: 72.8 us
  blocking collectives  38.4 us (52%)
  starting transfers between devices  14.7 us (20%)
  waiting for transfers between devices  8.8 us (12%)
  Pallas kernels  7.34 us (10%)
  local copies, waits for them, and re-layouts  2.79 us (4%)
    all_to_all x1, blocking collectives, exchange(): got = lax.all_to_all(sent, axis, split_axis=0, concat_axis=0, tiled=True)  25.1 us
    all_gather x1, blocking collectives, shards(): gathered = lax.all_gather(sums, 'red', axis=0)  13.4 us
    all_to_all x1, starting transfers between devices, exchange(): got = lax.all_to_all(sent, axis, split_axis=0, concat_axis=0, tiled=True)  8.1 us
    pallas_call x6, Pallas kernels, call(): pl.pallas_call(body, out_shape=outs if single else tuple(outs), scratch_s...  7.34 us
    all_to_all x1, starting transfers between devices, shards(): lax.all_to_all(table, 'red', split_axis=0, concat_axis=0, tiled=True)  6.64 us
    all_to_all x1, waiting for transfers between devices, exchange(): got = lax.all_to_all(sent, axis, split_axis=0, concat_axis=0, tiled=True)  6.26 us
    unnamed x22, local copies, waits for them, and re-layouts  2.79 us
    all_to_all x1, waiting for transfers between devices, shards(): lax.all_to_all(table, 'red', split_axis=0, concat_axis=0, tiled=True)  2.54 us
  transfers between devices with their start and end apart: 2, of which 2 were waited for; matrix products, arithmetic and copies ran while one was open for 0% of the time, Pallas kernels for 3%

profile of v1, /device:TPU:1, one launch (start us, length us, event | category | flops | bytes accessed | tf_op | source)
XLA Modules:
  0.0 72.8 jit_solution(8444285717905904942)
XLA Ops:
  0.6 0.0 copy-start
  0.6 1.2 %copy-done = bf16[512,1024]{1,0:T(8,128)(2,1)S(1)} copy-done((bf16[512,1024]{1,0:T(8,128)(2,1)S(1)}, bf16[512,1024]{1,0:T(8,128)(2,1)}, u32[]{:S(2)}) %copy-start) | copy-done | bytes 1048600
  1.9 0.0 copy-start.6
  1.9 0.9 %copy-done.6 = bf16[1024,3,4,4]{0,3,2,1:T(4,128)(2,1)S(1)} copy-done((bf16[1024,3,4,4]{0,3,2,1:T(4,128)(2,1)S(1)}, bf16[1024,3,4,4]{0,3,2,1:T(4,128)(2,1)}, u32[]{:S(2)}) %copy-start.6) | copy-done | bytes 98328
  2.8 0.0 copy-start.5
  2.8 1.1 %shard_map.130 = f32[4,48,128]{2,1,0:T(8,128)} custom-call(bf16[3,4,4,1024]{3,2,1,0:T(4,128)(2,1)S(1)} %bitcast.14, bf16[512,1024]{1,0:T(8,128)(2,1)S(1)} %copy-done), custom_call_target="tpu_custom_call" | custom-call | tf_op jit(solution)/shard_map/pallas_call | solution.py:232
  3.8 0.0 copy-start.4
  3.8 6.6 %all-to-all-start.1 = ((f32[4,48,128]{2,1,0:T(8,128)}), f32[4,48,128]{2,1,0:T(8,128)S(1)}, u32[]{:S(2)}, u32[]{:S(2)}) async-start(f32[4,48,128]{2,1,0:T(8,128)} %shard_map.130), calls=%async_computation.1 | async-start | bytes 196608 | tf_op jit(solution)/shard_map/all_to_all | solution.py:275
  10.5 0.0 copy-start.10
  10.5 0.0 copy-done.5
  10.5 0.0 copy-done.4
  10.5 0.6 copy-done.10
  11.1 0.0 copy-start.8
  11.1 0.0 copy-start.9
  11.1 0.1 shard_map.129
  11.3 2.5 %all-to-all-done.1.parts_ref = f32[4,48,128]{2,1,0:T(8,128)S(1)} async-done(((f32[4,48,128]{2,1,0:T(8,128)}), f32[4,48,128]{2,1,0:T(8,128)S(1)}, u32[]{:S(2)}, u32[]{:S(2)}) %all-to-all-start.1) | async-done | bytes 98336 | tf_op jit(solution)/shard_map/all_to_all | solution.py:275
  13.8 0.0 copy-start.2
  13.8 0.0 copy-start.3
  13.8 0.0 copy-start.7
  13.8 25.1 %all_to_all.15 = f32[64,1,1152]{2,1,0:T(1,128)S(1)} all-to-all(f32[64,1,1152]{2,1,0:T(1,128)S(1)} %bitcast.12), channel_id=1, replica_groups=mesh['seq'=64,'red'=4] {'seq'}, dimensions={0} | all-to-all | bytes 589824 | tf_op jit(solution)/shard_map/all_to_all | solution.py:246
  38.9 0.0 copy-done.8
  38.9 0.0 copy-done.9
  38.9 0.0 copy-done.2
  38.9 0.0 copy-done.3
  38.9 0.0 copy-done.7
  38.9 3.3 %shard_map.131 = (f32[1280,128]{1,0:T(8,128)}, f32[1024,128]{1,0:T(8,128)S(1)}) custom-call(f32[576,128]{1,0:T(8,128)S(1)} %bitcast.9, f32[4,48,128]{2,1,0:T(8,128)S(1)} %all-to-all-done.1.parts_ref, bf16[128,192]{1,0:T(8,128)(2,1)S(1)} %copy-done.8, bf16[64,384]{1,0:T(8,128)(2,1)S(1)} %copy-done.9, f32[2,64,128]{2,1,0:T(8,128)S(1)} %copy-done.7, ...), custom_call_target="tpu_custom_call" | custom-call | tf_op jit(solution)/shard_map/pallas_call | solution.py:232
  42.3 0.0 copy-start.1
  42.3 8.1 %all-to-all-start.2 = ((f32[64,1,2560]{2,1,0:T(1,128)}), f32[64,1,2560]{2,1,0:T(1,128)S(1)}, u32[]{:S(2)}, u32[]{:S(2)}) async-start(f32[64,1,2560]{2,1,0:T(1,128)} %bitcast.4), calls=%async_computation.2 | async-start | bytes 1310720 | tf_op jit(solution)/shard_map/all_to_all | solution.py:246
  50.4 0.9 %shard_map.133 = f32[64,128]{1,0:T(8,128)S(1)} custom-call(f32[576,128]{1,0:T(8,128)S(1)} %bitcast.10, f32[1024,128]{1,0:T(8,128)S(1)} %get-tuple-element.13.grads_ref), custom_call_target="tpu_custom_call" | custom-call | tf_op jit(solution)/shard_map/pallas_call | solution.py:232
  51.2 13.4 %all-gather = f32[256,128]{1,0:T(8,128)S(1)} all-gather(f32[64,128]{1,0:T(8,128)S(1)} %shard_map.133), channel_id=2, replica_groups=mesh['seq'=64,'red'=4] {'red'}, dimensions={0}, use_global_device_ids=true | all-gather | bytes 163840 | tf_op jit(solution)/shard_map/all_gather | solution.py:293
  64.6 0.0 copy-done.1
  64.6 1.0 %shard_map.134 = f32[3,4,4,1024]{3,2,1,0:T(4,128)} custom-call(f32[4,64,128]{2,1,0:T(8,128)S(1)} %bitcast.13, bf16[512,1024]{1,0:T(8,128)(2,1)S(1)} %copy-done.1), custom_call_target="tpu_custom_call" | custom-call | tf_op jit(solution)/shard_map/pallas_call | solution.py:232
  65.6 6.3 %all-to-all-done.2 = f32[64,1,2560]{2,1,0:T(1,128)S(1)} async-done(((f32[64,1,2560]{2,1,0:T(1,128)}), f32[64,1,2560]{2,1,0:T(1,128)S(1)}, u32[]{:S(2)}, u32[]{:S(2)}) %all-to-all-start.2) | async-done | bytes 655392 | tf_op jit(solution)/shard_map/all_to_all | solution.py:246
  71.8 0.9 %shard_map.132 = (f32[128,256]{1,0:T(8,128)}, f32[128,256]{1,0:T(8,128)}, bf16[3,128,256]{2,1,0:T(8,128)(2,1)}) custom-call(f32[1280,128]{1,0:T(8,128)S(1)} %bitcast.11), custom_call_target="tpu_custom_call" | custom-call | tf_op jit(solution)/shard_map/pallas_call | solution.py:232
Async XLA Ops:
  0.6 1.2 %copy-start = (bf16[512,1024]{1,0:T(8,128)(2,1)S(1)}, bf16[512,1024]{1,0:T(8,128)(2,1)}, u32[]{:S(2)}) copy-start(bf16[512,1024]{1,0:T(8,128)(2,1)} %emb_ref.3) | copy-start | bytes 3145732
  1.9 0.9 %copy-start.6 = (bf16[1024,3,4,4]{0,3,2,1:T(4,128)(2,1)S(1)}, bf16[1024,3,4,4]{0,3,2,1:T(4,128)(2,1)}, u32[]{:S(2)}) copy-start(bf16[1024,3,4,4]{0,3,2,1:T(4,128)(2,1)} %param.12) | copy-start | bytes 294916
  2.8 7.7 %copy-start.5 = (f32[128,256]{1,0:T(8,128)S(1)}, f32[128,256]{1,0:T(8,128)}, u32[]{:S(2)}) copy-start(f32[128,256]{1,0:T(8,128)} %cot_ref.1) | copy-start | bytes 393220
  3.8 6.7 %copy-start.4 = (f32[128,256]{1,0:T(8,128)S(1)}, f32[128,256]{1,0:T(8,128)}, u32[]{:S(2)}) copy-start(f32[128,256]{1,0:T(8,128)} %filt_ref.1) | copy-start | bytes 393220
  3.8 10.0 %all-to-all-start.1 = ((f32[4,48,128]{2,1,0:T(8,128)}), f32[4,48,128]{2,1,0:T(8,128)S(1)}, u32[]{:S(2)}, u32[]{:S(2)}) async-start(f32[4,48,128]{2,1,0:T(8,128)} %shard_map.130), calls=%async_computation.1 | async-start | bytes 196608 | tf_op jit(solution)/shard_map/all_to_all | solution.py:275
  10.5 0.7 copy-start.10
  11.1 27.8 %copy-start.8 = (bf16[128,192]{1,0:T(8,128)(2,1)S(1)}, bf16[128,192]{1,0:T(8,128)(2,1)}, u32[]{:S(2)}) copy-start(bf16[128,192]{1,0:T(8,128)(2,1)} %constant.10.clone.first_ref) | copy-start | bytes 147460
  11.1 27.8 %copy-start.9 = (bf16[64,384]{1,0:T(8,128)(2,1)S(1)}, bf16[64,384]{1,0:T(8,128)(2,1)}, u32[]{:S(2)}) copy-start(bf16[64,384]{1,0:T(8,128)(2,1)} %constant.11.clone.last_ref) | copy-start | bytes 147460
  13.8 25.1 %copy-start.2 = (bf16[2,256,256]{2,1,0:T(8,128)(2,1)S(1)}, bf16[2,256,256]{2,1,0:T(8,128)(2,1)}, u32[]{:S(2)}) copy-start(bf16[2,256,256]{2,1,0:T(8,128)(2,1)} %constant.14.clone.backward_ref) | copy-start | bytes 786436
  13.8 25.1 %copy-start.3 = (bf16[2,256,256]{2,1,0:T(8,128)(2,1)S(1)}, bf16[2,256,256]{2,1,0:T(8,128)(2,1)}, u32[]{:S(2)}) copy-start(bf16[2,256,256]{2,1,0:T(8,128)(2,1)} %constant.13.clone.forward_ref) | copy-start | bytes 786436
  13.8 25.1 %copy-start.7 = (f32[2,64,128]{2,1,0:T(8,128)S(1)}, f32[2,64,128]{2,1,0:T(8,128)}, u32[]{:S(2)}) copy-start(f32[2,64,128]{2,1,0:T(8,128)} %constant.12.clone.twiddle_ref) | copy-start | bytes 196612
  42.3 22.3 %copy-start.1 = (bf16[512,1024]{1,0:T(8,128)(2,1)S(1)}, bf16[512,1024]{1,0:T(8,128)(2,1)}, u32[]{:S(2)}) copy-start(bf16[512,1024]{1,0:T(8,128)(2,1)} %emb_ref.3) | copy-start | bytes 3145732
  42.3 29.6 %all-to-all-start.2 = ((f32[64,1,2560]{2,1,0:T(1,128)}), f32[64,1,2560]{2,1,0:T(1,128)S(1)}, u32[]{:S(2)}, u32[]{:S(2)}) async-start(f32[64,1,2560]{2,1,0:T(1,128)} %bitcast.4), calls=%async_computation.2 | async-start | bytes 1310720 | tf_op jit(solution)/shard_map/all_to_all | solution.py:246

commit v2 on v1

--- a/solution.py
+++ b/solution.py
@@ -80,7 +80,8 @@
     table = dot_last(rows_ref[...].astype(BF16), emb_ref[...])
     for q in range(reds):
         for part in range(table.shape[1] // LANES):
-            out_ref[q, part * wide : (part + 1) * wide, :] = table[
+            at = q * table.shape[1] // LANES * wide + part * wide
+            out_ref[at : at + wide, :] = table[
                 q * wide : (q + 1) * wide, part * LANES : (part + 1) * LANES
             ]
 
@@ -93,18 +94,20 @@
 
 
 def conv_kernel(
-    scale, in_ref, parts_ref, first_ref, last_ref, twiddle_ref, forward_ref, backward_ref, out_ref, grads_ref
+    scale, place_ref, in_ref, parts_ref, first_ref, last_ref, twiddle_ref, forward_ref, backward_ref, out_ref, grads_ref
 ):
-    reds, table_rows, _ = parts_ref.shape
+    reds = parts_ref.shape[0]
+    table_rows = parts_ref.shape[1] // reds
     wide = 3 * OWN
     groups = table_rows // wide
+    own_rows = pl.ds(pl.multiple_of(place_ref[0] * table_rows, 8), table_rows)
 
     def received(row):
         return in_ref[pl.ds(row, BLOCKS, stride=IN_ROWS), :]
 
-    table = parts_ref[0]
+    table = parts_ref[0, own_rows, :]
     for q in range(1, reds):
-        table = table + parts_ref[q]
+        table = table + parts_ref[q, own_rows, :]
     ids = received(2 * OWN).astype(jnp.int32)
     lane = ids & (LANES - 1)
     group = ids >> 7
@@ -227,10 +230,12 @@
             filter_ref[...] = value
 
 
-def call(body, outs, scratch, *operands):
+def call(body, outs, scratch, *operands, scalars=0):
     single = not isinstance(outs, (list, tuple))
+    spaces = [pltpu.SMEM] * scalars + [pltpu.VMEM] * (len(operands) - scalars)
     return pl.pallas_call(
         body,
+        in_specs=[pl.BlockSpec(memory_space=space) for space in spaces],
         out_shape=outs if single else tuple(outs),
         scratch_shapes=scratch,
         compiler_params=pltpu.CompilerParams(vmem_limit_bytes=48 * 2**20),
@@ -267,20 +272,22 @@
     arrived = exchange(packed, "seq", BLOCKS, IN_ROWS)
     table = call(
         table_kernel,
-        shape((reds, groups * branches * piece, LANES)),
+        shape((reds * groups * branches * piece, LANES)),
         [pltpu.VMEM((reds * branches * piece, width_rows), F32)],
         proj_weight.transpose(1, 2, 3, 0),
         embedding,
     )
-    parts = lax.all_to_all(table, "red", split_axis=0, concat_axis=0, tiled=True)
+    parts = lax.all_gather(table, "red", axis=0)
     constants = [jnp.asarray(c) for c in transform_constants()]
     results, grads = call(
         functools.partial(conv_kernel, scale),
         [shape((BLOCKS * OUT_ROWS, LANES)), shape((BLOCKS * 16, LANES))],
         [],
+        lax.axis_index("red").reshape(1),
         arrived,
         parts,
         *constants,
+        scalars=1,
     )
     returned = exchange(results, "seq", BLOCKS, OUT_ROWS)
     sums = call(

time: 73.2 us -> 68.6 us (0.937)
  the two profiles are of different devices: /device:TPU:1 before, /device:TPU:32 now
where the time goes in v2:
time: 68.6 us; the launch traced here: 67.9 us
  blocking collectives  25.6 us (37%)
  starting transfers between devices  19.4 us (28%)
  waiting for transfers between devices  12.2 us (18%)
  Pallas kernels  7.4 us (11%)
  local copies, waits for them, and re-layouts  2.59 us (4%)
  between operations  0.77 us (1%)
    all_to_all x2, starting transfers between devices, exchange(): got = lax.all_to_all(sent, axis, split_axis=0, concat_axis=0, tiled=True)  19.4 us
    all_gather x1, blocking collectives, shards(): gathered = lax.all_gather(sums, 'red', axis=0)  16 us
    all_to_all x2, waiting for transfers between devices, exchange(): got = lax.all_to_all(sent, axis, split_axis=0, concat_axis=0, tiled=True)  12.2 us
    all_gather x1, blocking collectives, shards(): parts = lax.all_gather(table, 'red', axis=0)  9.57 us
    pallas_call x6, Pallas kernels, call(): pl.pallas_call(body, in_specs=[pl.BlockSpec(memory_space=space) for space...  7.4 us
    unnamed x20, local copies, waits for them, and re-layouts  2.59 us
  transfers between devices with their start and end apart: 2, of which 2 were waited for; matrix products, arithmetic and copies ran while one was open for 0% of the time, Pallas kernels for 3%

profile of v2, /device:TPU:32, one launch (start us, length us, event | category | flops | bytes accessed | tf_op | source)
XLA Modules:
  0.0 67.9 jit_solution(17801862245783222360)
XLA Ops:
  0.6 0.0 copy-start
  0.6 0.0 copy-start.3
  0.7 1.0 %copy-done.3 = f32[128,256]{1,0:T(8,128)S(1)} copy-done((f32[128,256]{1,0:T(8,128)S(1)}, f32[128,256]{1,0:T(8,128)}, u32[]{:S(2)}) %copy-start.3) | copy-done | bytes 131096
  1.6 0.0 copy-start.4
  1.6 0.9 %copy-done.4 = f32[128,256]{1,0:T(8,128)S(1)} copy-done((f32[128,256]{1,0:T(8,128)S(1)}, f32[128,256]{1,0:T(8,128)}, u32[]{:S(2)}) %copy-start.4) | copy-done | bytes 131096
  2.5 0.0 copy-start.9
  2.5 0.7 copy-done.9
  3.2 0.9 %shard_map.129 = f32[576,128]{1,0:T(8,128)} custom-call(s32[1,128]{1,0:T(1,128)S(1)} %bitcast.17, f32[128,256]{1,0:T(8,128)S(1)} %copy-done.3, f32[128,256]{1,0:T(8,128)S(1)} %copy-done.4), custom_call_target="tpu_custom_call" | custom-call | tf_op jit(solution)/shard_map/pallas_call | solution.py:236
  4.0 0.0 copy-start.5
  4.0 13.8 %all-to-all-start = ((f32[64,1,1152]{2,1,0:T(1,128)}), f32[64,1,1152]{2,1,0:T(1,128)S(1)}, u32[]{:S(2)}, u32[]{:S(2)}) async-start(f32[64,1,1152]{2,1,0:T(1,128)} %bitcast.2), calls=%async_computation | async-start | bytes 589824 | tf_op jit(solution)/shard_map/all_to_all | solution.py:251
  17.9 0.0 copy-done
  17.9 0.0 copy-done.5
  17.9 0.0 copy-start.2
  17.9 0.4 shard_map.130
  18.3 0.0 copy-start.1
  18.4 0.0 copy-start.6
  18.4 0.0 copy-start.7
  18.4 0.0 copy-start.8
  18.4 9.6 %all-gather = f32[768,128]{1,0:T(8,128)S(1)} all-gather(f32[192,128]{1,0:T(8,128)S(1)} %shard_map.130), channel_id=2, replica_groups=mesh['seq'=64,'red'=4] {'red'}, dimensions={0}, use_global_device_ids=true | all-gather | bytes 491520 | tf_op jit(solution)/shard_map/all_gather | solution.py:280
  28.0 6.8 %all-to-all-done = f32[64,1,1152]{2,1,0:T(1,128)S(1)} async-done(((f32[64,1,1152]{2,1,0:T(1,128)}), f32[64,1,1152]{2,1,0:T(1,128)S(1)}, u32[]{:S(2)}, u32[]{:S(2)}) %all-to-all-start) | async-done | bytes 294944 | tf_op jit(solution)/shard_map/all_to_all | solution.py:251
  34.7 0.0 copy-done.2
  34.7 0.0 copy-done.1
  34.7 0.0 copy-done.6
  34.7 0.0 copy-done.7
  34.7 0.0 copy-done.8
  34.8 3.3 %shard_map.131 = (f32[1280,128]{1,0:T(8,128)}, f32[1024,128]{1,0:T(8,128)S(1)}) custom-call(s32[1]{0:T(128)} %bitcast.place_ref, f32[576,128]{1,0:T(8,128)S(1)} %bitcast.11, f32[4,192,128]{2,1,0:T(8,128)S(1)} %bitcast.14, bf16[128,192]{1,0:T(8,128)(2,1)S(1)} %copy-done.7, bf16[64,384]{1,0:T(8,128)(2,1)S(1)} %copy-done.8, f32[2,64,128]{2,1,0:T(8,128)S(1)} %copy-done.6, ...), custom_call_target="tpu_custom_call" | custom-call | tf_op jit(solution)/shard_map/pallas_call | solution.py:236
  38.1 5.6 %all-to-all-start.1 = ((f32[64,1,2560]{2,1,0:T(1,128)}), f32[64,1,2560]{2,1,0:T(1,128)S(1)}, u32[]{:S(2)}, u32[]{:S(2)}) async-start(f32[64,1,2560]{2,1,0:T(1,128)} %bitcast.6), calls=%async_computation.1 | async-start | bytes 1310720 | tf_op jit(solution)/shard_map/all_to_all | solution.py:251
  43.7 0.8 %shard_map.133 = f32[64,128]{1,0:T(8,128)S(1)} custom-call(f32[576,128]{1,0:T(8,128)S(1)} %bitcast.12, f32[1024,128]{1,0:T(8,128)S(1)} %get-tuple-element.13.grads_ref), custom_call_target="tpu_custom_call" | custom-call | tf_op jit(solution)/shard_map/pallas_call | solution.py:236
  44.5 16.0 %all-gather.1 = f32[256,128]{1,0:T(8,128)S(1)} all-gather(f32[64,128]{1,0:T(8,128)S(1)} %shard_map.133), channel_id=3, replica_groups=mesh['seq'=64,'red'=4] {'red'}, dimensions={0}, use_global_device_ids=true | all-gather | bytes 163840 | tf_op jit(solution)/shard_map/all_gather | solution.py:300
  60.5 1.0 %shard_map.134 = f32[3,4,4,1024]{3,2,1,0:T(4,128)} custom-call(f32[4,64,128]{2,1,0:T(8,128)S(1)} %bitcast.15, bf16[512,1024]{1,0:T(8,128)(2,1)S(1)} %copy-done), custom_call_target="tpu_custom_call" | custom-call | tf_op jit(solution)/shard_map/pallas_call | solution.py:236
  61.5 5.5 %all-to-all-done.1 = f32[64,1,2560]{2,1,0:T(1,128)S(1)} async-done(((f32[64,1,2560]{2,1,0:T(1,128)}), f32[64,1,2560]{2,1,0:T(1,128)S(1)}, u32[]{:S(2)}, u32[]{:S(2)}) %all-to-all-start.1) | async-done | bytes 655392 | tf_op jit(solution)/shard_map/all_to_all | solution.py:251
  67.0 0.9 %shard_map.132 = (f32[128,256]{1,0:T(8,128)}, f32[128,256]{1,0:T(8,128)}, bf16[3,128,256]{2,1,0:T(8,128)(2,1)}) custom-call(f32[1280,128]{1,0:T(8,128)S(1)} %bitcast.13), custom_call_target="tpu_custom_call" | custom-call | tf_op jit(solution)/shard_map/pallas_call | solution.py:236
Async XLA Ops:
  0.6 17.2 %copy-start = (bf16[512,1024]{1,0:T(8,128)(2,1)S(1)}, bf16[512,1024]{1,0:T(8,128)(2,1)}, u32[]{:S(2)}) copy-start(bf16[512,1024]{1,0:T(8,128)(2,1)} %emb_ref.3) | copy-start | bytes 3145732
  0.6 1.0 %copy-start.3 = (f32[128,256]{1,0:T(8,128)S(1)}, f32[128,256]{1,0:T(8,128)}, u32[]{:S(2)}) copy-start(f32[128,256]{1,0:T(8,128)} %filt_ref.1) | copy-start | bytes 393220
  1.6 0.9 %copy-start.4 = (f32[128,256]{1,0:T(8,128)S(1)}, f32[128,256]{1,0:T(8,128)}, u32[]{:S(2)}) copy-start(f32[128,256]{1,0:T(8,128)} %cot_ref.1) | copy-start | bytes 393220
  2.5 0.7 copy-start.9
  4.0 13.8 %copy-start.5 = (bf16[1024,3,4,4]{0,3,2,1:T(4,128)(2,1)S(1)}, bf16[1024,3,4,4]{0,3,2,1:T(4,128)(2,1)}, u32[]{:S(2)}) copy-start(bf16[1024,3,4,4]{0,3,2,1:T(4,128)(2,1)} %param.12) | copy-start | bytes 294916
  4.0 30.7 %all-to-all-start = ((f32[64,1,1152]{2,1,0:T(1,128)}), f32[64,1,1152]{2,1,0:T(1,128)S(1)}, u32[]{:S(2)}, u32[]{:S(2)}) async-start(f32[64,1,1152]{2,1,0:T(1,128)} %bitcast.2), calls=%async_computation | async-start | bytes 589824 | tf_op jit(solution)/shard_map/all_to_all | solution.py:251
  17.9 16.8 %copy-start.2 = (bf16[2,256,256]{2,1,0:T(8,128)(2,1)S(1)}, bf16[2,256,256]{2,1,0:T(8,128)(2,1)}, u32[]{:S(2)}) copy-start(bf16[2,256,256]{2,1,0:T(8,128)(2,1)} %constant.17.clone.forward_ref) | copy-start | bytes 786436
  18.3 16.4 %copy-start.1 = (bf16[2,256,256]{2,1,0:T(8,128)(2,1)S(1)}, bf16[2,256,256]{2,1,0:T(8,128)(2,1)}, u32[]{:S(2)}) copy-start(bf16[2,256,256]{2,1,0:T(8,128)(2,1)} %constant.18.clone.backward_ref) | copy-start | bytes 786436
  18.4 16.4 %copy-start.6 = (f32[2,64,128]{2,1,0:T(8,128)S(1)}, f32[2,64,128]{2,1,0:T(8,128)}, u32[]{:S(2)}) copy-start(f32[2,64,128]{2,1,0:T(8,128)} %constant.16.clone.twiddle_ref) | copy-start | bytes 196612
  18.4 16.4 %copy-start.7 = (bf16[128,192]{1,0:T(8,128)(2,1)S(1)}, bf16[128,192]{1,0:T(8,128)(2,1)}, u32[]{:S(2)}) copy-start(bf16[128,192]{1,0:T(8,128)(2,1)} %constant.14.clone.first_ref) | copy-start | bytes 147460
  18.4 16.4 %copy-start.8 = (bf16[64,384]{1,0:T(8,128)(2,1)S(1)}, bf16[64,384]{1,0:T(8,128)(2,1)}, u32[]{:S(2)}) copy-start(bf16[64,384]{1,0:T(8,128)(2,1)} %constant.15.clone.last_ref) | copy-start | bytes 147460
  38.1 28.9 %all-to-all-start.1 = ((f32[64,1,2560]{2,1,0:T(1,128)}), f32[64,1,2560]{2,1,0:T(1,128)S(1)}, u32[]{:S(2)}, u32[]{:S(2)}) async-start(f32[64,1,2560]{2,1,0:T(1,128)} %bitcast.6), calls=%async_computation.1 | async-start | bytes 1310720 | tf_op jit(solution)/shard_map/all_to_all | solution.py:251

commit v3 on v1

--- a/solution.py
+++ b/solution.py
@@ -58,31 +58,37 @@
     return lax.dot_general(left, right, (((1,), (1,)), ((), ())), preferred_element_type=F32)
 
 
-def pack_kernel(ids_ref, filt_ref, cot_ref, out_ref, turn_ref):
-    for number, ref in enumerate((filt_ref, cot_ref)):
+def pack_kernel(filt_hbm, cot_hbm, ids_hbm, out_ref, filt, cot, ids, turn_ref, sems):
+    pairs = ((filt_hbm, filt), (cot_hbm, cot), (ids_hbm, ids))
+    copies = [pltpu.make_async_copy(source, kept, sems.at[n]) for n, (source, kept) in enumerate(pairs)]
+    for copy in copies:
+        copy.start()
+    for number, ref in enumerate((filt, cot)):
+        copies[number].wait()
         turn_ref[...] = ref[...].T
         for c in range(OWN):
             out_ref[pl.ds(number * OWN + c, BLOCKS, stride=IN_ROWS), :] = turn_ref[
                 pl.ds(c, BLOCKS, stride=OWN), :
             ]
-    out_ref[pl.ds(2 * OWN, BLOCKS, stride=IN_ROWS), :] = jnp.broadcast_to(
-        ids_ref[...].astype(F32), (BLOCKS, LANES)
-    )
-
-
-def table_kernel(proj_ref, emb_ref, out_ref, rows_ref):
+    copies[2].wait()
+    out_ref[pl.ds(2 * OWN, BLOCKS, stride=IN_ROWS), :] = jnp.broadcast_to(ids[...].astype(F32), (BLOCKS, LANES))
+
+
+def table_kernel(proj_ref, emb_ref, *refs):
+    *out_refs, rows_ref, table_ref = refs
     branches, reds, piece, _ = proj_ref.shape
     wide = branches * piece
+    rows_ref[...] = jnp.zeros_like(rows_ref)
     for q in range(reds):
         for b in range(branches):
-            at = q * wide + b * piece
+            at = q * 16 + b * piece
             rows_ref[at : at + piece, :] = proj_ref[b, q].astype(F32)
-    table = dot_last(rows_ref[...].astype(BF16), emb_ref[...])
-    for q in range(reds):
-        for part in range(table.shape[1] // LANES):
-            out_ref[q, part * wide : (part + 1) * wide, :] = table[
-                q * wide : (q + 1) * wide, part * LANES : (part + 1) * LANES
-            ]
+    table_ref[...] = dot_last(rows_ref[...].astype(BF16), emb_ref[...])
+    place = lax.axis_index("red")
+    for apart, out_ref in enumerate(out_refs):
+        rows = table_ref[pl.ds(pl.multiple_of((place ^ apart) * 16, 16), 16), :]
+        for part in range(rows.shape[1] // LANES):
+            out_ref[part * wide : (part + 1) * wide, :] = rows[:wide, part * LANES : (part + 1) * LANES]
 
 
 def right_product(value, matrix_ref):
@@ -93,18 +99,15 @@
 
 
 def conv_kernel(
-    scale, in_ref, parts_ref, first_ref, last_ref, twiddle_ref, forward_ref, backward_ref, out_ref, grads_ref
+    scale, in_ref, part_0, part_1, part_2, part_3, first_ref, last_ref, twiddle_ref, forward_ref, backward_ref, out_ref, grads_ref
 ):
-    reds, table_rows, _ = parts_ref.shape
     wide = 3 * OWN
-    groups = table_rows // wide
+    groups = part_0.shape[0] // wide
 
     def received(row):
         return in_ref[pl.ds(row, BLOCKS, stride=IN_ROWS), :]
 
-    table = parts_ref[0]
-    for q in range(1, reds):
-        table = table + parts_ref[q]
+    table = (part_0[...] + part_1[...]) + (part_2[...] + part_3[...])
     ids = received(2 * OWN).astype(jnp.int32)
     lane = ids & (LANES - 1)
     group = ids >> 7
@@ -227,13 +230,14 @@
             filter_ref[...] = value
 
 
-def call(body, outs, scratch, *operands):
+def call(body, outs, scratch, *operands, space=pltpu.VMEM, limit=48 * 2**20):
     single = not isinstance(outs, (list, tuple))
     return pl.pallas_call(
         body,
+        in_specs=[pl.BlockSpec(memory_space=space)] * len(operands),
         out_shape=outs if single else tuple(outs),
         scratch_shapes=scratch,
-        compiler_params=pltpu.CompilerParams(vmem_limit_bytes=48 * 2**20),
+        compiler_params=pltpu.CompilerParams(vmem_limit_bytes=limit),
     )(*operands)
 
 
@@ -259,27 +263,37 @@
     packed = call(
         pack_kernel,
         shape((BLOCKS * IN_ROWS, LANES)),
-        [pltpu.VMEM((channels, LANES), F32)],
-        token_ids.reshape(1, positions),
+        [
+            pltpu.VMEM((positions, channels), F32),
+            pltpu.VMEM((positions, channels), F32),
+            pltpu.VMEM((1, positions), jnp.int32),
+            pltpu.VMEM((channels, LANES), F32),
+            pltpu.SemaphoreType.DMA((3,)),
+        ],
         filters,
         cotangent,
+        token_ids.reshape(1, positions),
+        space=pl.ANY,
+        limit=60 * 2**20,
     )
     arrived = exchange(packed, "seq", BLOCKS, IN_ROWS)
-    table = call(
+    parts = call(
         table_kernel,
-        shape((reds, groups * branches * piece, LANES)),
-        [pltpu.VMEM((reds * branches * piece, width_rows), F32)],
+        [shape((groups * branches * piece, LANES))] * reds,
+        [pltpu.VMEM((reds * 16, width_rows), F32), pltpu.VMEM((reds * 16, vocabulary), F32)],
         proj_weight.transpose(1, 2, 3, 0),
         embedding,
     )
-    parts = lax.all_to_all(table, "red", split_axis=0, concat_axis=0, tiled=True)
+    parts = [parts[0]] + [
+        lax.ppermute(parts[apart], "red", [(q, q ^ apart) for q in range(reds)]) for apart in range(1, reds)
+    ]
     constants = [jnp.asarray(c) for c in transform_constants()]
     results, grads = call(
         functools.partial(conv_kernel, scale),
         [shape((BLOCKS * OUT_ROWS, LANES)), shape((BLOCKS * 16, LANES))],
         [],
         arrived,
-        parts,
+        *parts,
         *constants,
     )
     returned = exchange(results, "seq", BLOCKS, OUT_ROWS)

time: 73.2 us -> 65.3 us (0.89)
  the two profiles are of different devices: /device:TPU:1 before, /device:TPU:32 now
where the time goes in v3:
time: 65.3 us; the launch traced here: 65 us
  waiting for transfers between devices  21.1 us (32%)
  starting transfers between devices  20.4 us (31%)
  blocking collectives  14.2 us (22%)
  Pallas kernels  8.55 us (13%)
  between operations  0.78 us (1%)
    all_to_all x2, starting transfers between devices, exchange(): got = lax.all_to_all(sent, axis, split_axis=0, concat_axis=0, tiled=True)  18.4 us
    all_to_all x2, waiting for transfers between devices, exchange(): got = lax.all_to_all(sent, axis, split_axis=0, concat_axis=0, tiled=True)  16.5 us
    all_gather x1, blocking collectives, shards(): gathered = lax.all_gather(sums, 'red', axis=0)  14.2 us
    pallas_call x6, Pallas kernels, call(): pl.pallas_call(body, in_specs=[pl.BlockSpec(memory_space=space)] * len(op...  8.55 us
    ppermute x3, waiting for transfers between devices, shards(): lax.ppermute(parts[apart], 'red', [(q, q ^ apart) for q in range(reds)])  4.62 us
    ppermute x3, starting transfers between devices, shards(): lax.ppermute(parts[apart], 'red', [(q, q ^ apart) for q in range(reds)])  1.96 us
  transfers between devices with their start and end apart: 5, of which 3 were waited for; matrix products, arithmetic and copies ran while one was open for 0% of the time, Pallas kernels for 4%

profile of v3, /device:TPU:32, one launch (start us, length us, event | category | flops | bytes accessed | tf_op | source)
XLA Modules:
  0.0 65.0 jit_solution(14736773657734447617)
XLA Ops:
  0.6 0.0 copy-start
  0.6 2.0 %shard_map.129 = f32[576,128]{1,0:T(8,128)} custom-call(f32[128,256]{1,0:T(8,128)} %filt_hbm.1, f32[128,256]{1,0:T(8,128)} %cot_hbm.1, s32[1,128]{1,0:T(1,128)} %bitcast.16), custom_call_target="tpu_custom_call" | custom-call | tf_op jit(solution)/shard_map/pallas_call | solution.py:235
  2.6 0.0 copy-start.3
  2.6 13.8 %all-to-all-start = ((f32[64,1,1152]{2,1,0:T(1,128)}), f32[64,1,1152]{2,1,0:T(1,128)S(1)}, u32[]{:S(2)}, u32[]{:S(2)}) async-start(f32[64,1,1152]{2,1,0:T(1,128)} %bitcast.14), calls=%async_computation | async-start | bytes 589824 | tf_op jit(solution)/shard_map/all_to_all | solution.py:250
  16.4 0.0 copy-done
  16.5 0.0 copy-done.3
  16.5 0.0 copy-start.1
  16.5 0.0 copy-start.2
  16.5 0.0 copy-start.4
  16.5 0.0 copy-start.5
  16.5 0.0 copy-start.6
  16.5 0.5 shard_map.130
  17.0 0.1 collective-permute-start
  17.1 1.1 %collective-permute-start.1 = (f32[48,128]{1,0:T(8,128)S(1)}, f32[48,128]{1,0:T(8,128)S(1)}, u32[]{:S(2)}, u32[]{:S(2)}) collective-permute-start(f32[48,128]{1,0:T(8,128)S(1)} %get-tuple-element.15), channel_id=1, source_target_pairs={{0,2},{1,3},{2,0},{3,1},{4,6},{5,7},{6,4},{7,5},{8,10},{9,11},{10,... | collective-permute-start | bytes 73736 | tf_op jit(solution)/shard_map/ppermute | solution.py:288
  18.2 0.8 %collective-permute-start.2 = (f32[48,128]{1,0:T(8,128)S(1)}, f32[48,128]{1,0:T(8,128)S(1)}, u32[]{:S(2)}, u32[]{:S(2)}) collective-permute-start(f32[48,128]{1,0:T(8,128)S(1)} %get-tuple-element.16), channel_id=1, source_target_pairs={{0,3},{1,2},{2,1},{3,0},{4,7},{5,6},{6,5},{7,4},{8,11},{9,10},{10,... | collective-permute-start | bytes 73736 | tf_op jit(solution)/shard_map/ppermute | solution.py:288
  19.0 0.0 collective-permute-done.part_1
  19.0 4.6 %collective-permute-done.1.part_2 = f32[48,128]{1,0:T(8,128)S(1)} collective-permute-done((f32[48,128]{1,0:T(8,128)S(1)}, f32[48,128]{1,0:T(8,128)S(1)}, u32[]{:S(2)}, u32[]{:S(2)}) %collective-permute-start.1) | collective-permute-done | bytes 24608 | tf_op jit(solution)/shard_map/ppermute | solution.py:288
  23.6 0.0 collective-permute-done.2.part_3
  23.6 9.3 %all-to-all-done = f32[64,1,1152]{2,1,0:T(1,128)S(1)} async-done(((f32[64,1,1152]{2,1,0:T(1,128)}), f32[64,1,1152]{2,1,0:T(1,128)S(1)}, u32[]{:S(2)}, u32[]{:S(2)}) %all-to-all-start) | async-done | bytes 294944 | tf_op jit(solution)/shard_map/all_to_all | solution.py:250
  32.9 0.0 copy-done.1
  32.9 0.0 copy-done.2
  32.9 0.0 copy-done.4
  32.9 0.0 copy-done.5
  32.9 0.0 copy-done.6
  32.9 3.3 %shard_map.131 = (f32[1280,128]{1,0:T(8,128)}, f32[1024,128]{1,0:T(8,128)S(1)}) custom-call(f32[576,128]{1,0:T(8,128)S(1)} %bitcast.9, f32[48,128]{1,0:T(8,128)S(1)} %get-tuple-element.13.part_0, f32[48,128]{1,0:T(8,128)S(1)} %collective-permute-done.part_1, f32[48,128]{1,0:T(8,128)S(1)} %collective-permute-done.1.part_2, ...), custom_call_target="tpu_custom_call" | custom-call | tf_op jit(solution)/shard_map/pallas_call | solution.py:235
  36.3 4.6 %all-to-all-start.1 = ((f32[64,1,2560]{2,1,0:T(1,128)}), f32[64,1,2560]{2,1,0:T(1,128)S(1)}, u32[]{:S(2)}, u32[]{:S(2)}) async-start(f32[64,1,2560]{2,1,0:T(1,128)} %bitcast.4), calls=%async_computation.1 | async-start | bytes 1310720 | tf_op jit(solution)/shard_map/all_to_all | solution.py:250
  40.9 0.8 %shard_map.133 = f32[64,128]{1,0:T(8,128)S(1)} custom-call(f32[576,128]{1,0:T(8,128)S(1)} %bitcast.10, f32[1024,128]{1,0:T(8,128)S(1)} %get-tuple-element.21.grads_ref), custom_call_target="tpu_custom_call" | custom-call | tf_op jit(solution)/shard_map/pallas_call | solution.py:235
  41.8 14.2 %all-gather = f32[256,128]{1,0:T(8,128)S(1)} all-gather(f32[64,128]{1,0:T(8,128)S(1)} %shard_map.133), channel_id=2, replica_groups=mesh['seq'=64,'red'=4] {'red'}, dimensions={0}, use_global_device_ids=true | all-gather | bytes 163840 | tf_op jit(solution)/shard_map/all_gather | solution.py:307
  55.9 1.0 %shard_map.134 = f32[3,4,4,1024]{3,2,1,0:T(4,128)} custom-call(f32[4,64,128]{2,1,0:T(8,128)S(1)} %bitcast.12, bf16[512,1024]{1,0:T(8,128)(2,1)S(1)} %copy-done), custom_call_target="tpu_custom_call" | custom-call | tf_op jit(solution)/shard_map/pallas_call | solution.py:235
  56.9 7.1 %all-to-all-done.1 = f32[64,1,2560]{2,1,0:T(1,128)S(1)} async-done(((f32[64,1,2560]{2,1,0:T(1,128)}), f32[64,1,2560]{2,1,0:T(1,128)S(1)}, u32[]{:S(2)}, u32[]{:S(2)}) %all-to-all-start.1) | async-done | bytes 655392 | tf_op jit(solution)/shard_map/all_to_all | solution.py:250
  64.1 0.9 %shard_map.132 = (f32[128,256]{1,0:T(8,128)}, f32[128,256]{1,0:T(8,128)}, bf16[3,128,256]{2,1,0:T(8,128)(2,1)}) custom-call(f32[1280,128]{1,0:T(8,128)S(1)} %bitcast.11), custom_call_target="tpu_custom_call" | custom-call | tf_op jit(solution)/shard_map/pallas_call | solution.py:235
Async XLA Ops:
  0.6 15.8 %copy-start = (bf16[512,1024]{1,0:T(8,128)(2,1)S(1)}, bf16[512,1024]{1,0:T(8,128)(2,1)}, u32[]{:S(2)}) copy-start(bf16[512,1024]{1,0:T(8,128)(2,1)} %emb_ref.3) | copy-start | bytes 3145732
  2.6 13.8 %copy-start.3 = (bf16[1024,3,4,4]{0,3,2,1:T(4,128)(2,1)S(1)}, bf16[1024,3,4,4]{0,3,2,1:T(4,128)(2,1)}, u32[]{:S(2)}) copy-start(bf16[1024,3,4,4]{0,3,2,1:T(4,128)(2,1)} %param.12) | copy-start | bytes 294916
  2.6 30.3 %all-to-all-start = ((f32[64,1,1152]{2,1,0:T(1,128)}), f32[64,1,1152]{2,1,0:T(1,128)S(1)}, u32[]{:S(2)}, u32[]{:S(2)}) async-start(f32[64,1,1152]{2,1,0:T(1,128)} %bitcast.14), calls=%async_computation | async-start | bytes 589824 | tf_op jit(solution)/shard_map/all_to_all | solution.py:250
  16.5 16.4 %copy-start.1 = (bf16[2,256,256]{2,1,0:T(8,128)(2,1)S(1)}, bf16[2,256,256]{2,1,0:T(8,128)(2,1)}, u32[]{:S(2)}) copy-start(bf16[2,256,256]{2,1,0:T(8,128)(2,1)} %constant.14.clone.backward_ref) | copy-start | bytes 786436
  16.5 16.4 %copy-start.2 = (bf16[2,256,256]{2,1,0:T(8,128)(2,1)S(1)}, bf16[2,256,256]{2,1,0:T(8,128)(2,1)}, u32[]{:S(2)}) copy-start(bf16[2,256,256]{2,1,0:T(8,128)(2,1)} %constant.13.clone.forward_ref) | copy-start | bytes 786436
  16.5 16.4 %copy-start.4 = (f32[2,64,128]{2,1,0:T(8,128)S(1)}, f32[2,64,128]{2,1,0:T(8,128)}, u32[]{:S(2)}) copy-start(f32[2,64,128]{2,1,0:T(8,128)} %constant.12.clone.twiddle_ref) | copy-start | bytes 196612
  16.5 16.4 %copy-start.5 = (bf16[128,192]{1,0:T(8,128)(2,1)S(1)}, bf16[128,192]{1,0:T(8,128)(2,1)}, u32[]{:S(2)}) copy-start(bf16[128,192]{1,0:T(8,128)(2,1)} %constant.10.clone.first_ref) | copy-start | bytes 147460
  16.5 16.4 %copy-start.6 = (bf16[64,384]{1,0:T(8,128)(2,1)S(1)}, bf16[64,384]{1,0:T(8,128)(2,1)}, u32[]{:S(2)}) copy-start(bf16[64,384]{1,0:T(8,128)(2,1)} %constant.11.clone.last_ref) | copy-start | bytes 147460
  17.0 2.0 %collective-permute-start = (f32[48,128]{1,0:T(8,128)S(1)}, f32[48,128]{1,0:T(8,128)S(1)}, u32[]{:S(2)}, u32[]{:S(2)}) collective-permute-start(f32[48,128]{1,0:T(8,128)S(1)} %get-tuple-element.14), channel_id=1, source_target_pairs={{0,1},{1,0},{2,3},{3,2},{4,5},{5,4},{6,7},{7,6},{8,9},{9,8},{10,11... | collective-permute-start | bytes 73736 | tf_op jit(solution)/shard_map/ppermute | solution.py:288
  17.1 6.5 %collective-permute-start.1 = (f32[48,128]{1,0:T(8,128)S(1)}, f32[48,128]{1,0:T(8,128)S(1)}, u32[]{:S(2)}, u32[]{:S(2)}) collective-permute-start(f32[48,128]{1,0:T(8,128)S(1)} %get-tuple-element.15), channel_id=1, source_target_pairs={{0,2},{1,3},{2,0},{3,1},{4,6},{5,7},{6,4},{7,5},{8,10},{9,11},{10,... | collective-permute-start | bytes 73736 | tf_op jit(solution)/shard_map/ppermute | solution.py:288
  18.2 5.4 %collective-permute-start.2 = (f32[48,128]{1,0:T(8,128)S(1)}, f32[48,128]{1,0:T(8,128)S(1)}, u32[]{:S(2)}, u32[]{:S(2)}) collective-permute-start(f32[48,128]{1,0:T(8,128)S(1)} %get-tuple-element.16), channel_id=1, source_target_pairs={{0,3},{1,2},{2,1},{3,0},{4,7},{5,6},{6,5},{7,4},{8,11},{9,10},{10,... | collective-permute-start | bytes 73736 | tf_op jit(solution)/shard_map/ppermute | solution.py:288
  36.3 27.8 %all-to-all-start.1 = ((f32[64,1,2560]{2,1,0:T(1,128)}), f32[64,1,2560]{2,1,0:T(1,128)S(1)}, u32[]{:S(2)}, u32[]{:S(2)}) async-start(f32[64,1,2560]{2,1,0:T(1,128)} %bitcast.4), calls=%async_computation.1 | async-start | bytes 1310720 | tf_op jit(solution)/shard_map/all_to_all | solution.py:250

commit v4 on v3

--- a/solution.py
+++ b/solution.py
@@ -58,6 +58,13 @@
     return lax.dot_general(left, right, (((1,), (1,)), ((), ())), preferred_element_type=F32)
 
 
+def in_blocks_order(in_ref, row):
+    halves = [
+        in_ref[pl.ds(place * IN_ROWS + row, BLOCKS // 2, stride=IN_ROWS), :] for place in (BLOCKS // 2, 0)
+    ]
+    return jnp.concatenate(halves, axis=0)
+
+
 def pack_kernel(filt_hbm, cot_hbm, ids_hbm, out_ref, filt, cot, ids, turn_ref, sems):
     pairs = ((filt_hbm, filt), (cot_hbm, cot), (ids_hbm, ids))
     copies = [pltpu.make_async_copy(source, kept, sems.at[n]) for n, (source, kept) in enumerate(pairs)]
@@ -67,9 +74,12 @@
         copies[number].wait()
         turn_ref[...] = ref[...].T
         for c in range(OWN):
-            out_ref[pl.ds(number * OWN + c, BLOCKS, stride=IN_ROWS), :] = turn_ref[
-                pl.ds(c, BLOCKS, stride=OWN), :
-            ]
+            for half in range(2):
+                block = half * BLOCKS // 2
+                place = (1 - half) * BLOCKS // 2
+                out_ref[pl.ds(place * IN_ROWS + number * OWN + c, BLOCKS // 2, stride=IN_ROWS), :] = turn_ref[
+                    pl.ds(block * OWN + c, BLOCKS // 2, stride=OWN), :
+                ]
     copies[2].wait()
     out_ref[pl.ds(2 * OWN, BLOCKS, stride=IN_ROWS), :] = jnp.broadcast_to(ids[...].astype(F32), (BLOCKS, LANES))
 
@@ -105,7 +115,7 @@
     groups = part_0.shape[0] // wide
 
     def received(row):
-        return in_ref[pl.ds(row, BLOCKS, stride=IN_ROWS), :]
+        return in_blocks_order(in_ref, row)
 
     table = (part_0[...] + part_1[...]) + (part_2[...] + part_3[...])
     ids = received(2 * OWN).astype(jnp.int32)
@@ -176,7 +186,7 @@
 
 
 def sums_kernel(in_ref, grads_ref, out_ref, ids_ref):
-    ids_ref[...] = in_ref[pl.ds(2 * OWN, BLOCKS, stride=IN_ROWS), :].astype(jnp.int32)
+    ids_ref[...] = in_blocks_order(in_ref, 2 * OWN).astype(jnp.int32)
     groups = out_ref.shape[0] // 16
     total = jnp.zeros(out_ref.shape, F32)
     for pair in range(BLOCKS // 2):
@@ -245,9 +255,10 @@
     return jax.ShapeDtypeStruct(dims, dtype)
 
 
-def exchange(value, axis, pieces, rows):
+def exchange(value, axis, pieces, rows, first=0):
+    order = [(first + place) % pieces for place in range(pieces)]
     sent = value.reshape(pieces, 1, rows * LANES)
-    got = lax.all_to_all(sent, axis, split_axis=0, concat_axis=0, tiled=True)
+    got = lax.all_to_all(sent, axis, split_axis=0, concat_axis=0, tiled=True, axis_index_groups=[order])
     return got.reshape(pieces * rows, LANES)
 
 
@@ -276,7 +287,7 @@
         space=pl.ANY,
         limit=60 * 2**20,
     )
-    arrived = exchange(packed, "seq", BLOCKS, IN_ROWS)
+    arrived = exchange(packed, "seq", BLOCKS, IN_ROWS, first=BLOCKS // 2)
     parts = call(
         table_kernel,
         [shape((groups * branches * piece, LANES))] * reds,

time: 65.3 us -> 62.5 us (0.957)
  starting transfers between devices: 20.4 us -> 25.9 us
  blocking collectives: 14.2 us -> 9.99 us
  waiting for transfers between devices: 21.1 us -> 17 us
    all_to_all x2, starting transfers between devices: 18.4 us -> 23.9 us  [exchange(): lax.all_to_all(sent, axis, split_axis=0, concat_axis=0, tiled=True, axis_...]
    all_to_all x2, waiting for transfers between devices: 16.5 us -> 11.9 us  [exchange(): lax.all_to_all(sent, axis, split_axis=0, concat_axis=0, tiled=True, axis_...]
    all_gather x1, blocking collectives: 14.2 us -> 9.99 us  [shards(): gathered = lax.all_gather(sums, 'red', axis=0)]
where the time goes in v4:
time: 62.5 us; the launch traced here: 62.2 us
  starting transfers between devices  25.9 us (41%)
  waiting for transfers between devices  17 us (27%)
  blocking collectives  9.99 us (16%)
  Pallas kernels  8.55 us (14%)
  between operations  0.78 us (1%)
    all_to_all x2, starting transfers between devices, exchange(): lax.all_to_all(sent, axis, split_axis=0, concat_axis=0, tiled=True, axis_...  23.9 us
    all_to_all x2, waiting for transfers between devices, exchange(): lax.all_to_all(sent, axis, split_axis=0, concat_axis=0, tiled=True, axis_...  11.9 us
    all_gather x1, blocking collectives, shards(): gathered = lax.all_gather(sums, 'red', axis=0)  9.99 us
    pallas_call x6, Pallas kernels, call(): pl.pallas_call(body, in_specs=[pl.BlockSpec(memory_space=space)] * len(op...  8.55 us
    ppermute x3, waiting for transfers between devices, shards(): lax.ppermute(parts[apart], 'red', [(q, q ^ apart) for q in range(reds)])  5.07 us
    ppermute x3, starting transfers between devices, shards(): lax.ppermute(parts[apart], 'red', [(q, q ^ apart) for q in range(reds)])  1.96 us
  transfers between devices with their start and end apart: 5, of which 3 were waited for; matrix products, arithmetic and copies ran while one was open for 0% of the time, Pallas kernels for 4%

profile of v4, /device:TPU:32, one launch (start us, length us, event | category | flops | bytes accessed | tf_op | source)
XLA Modules:
  0.0 62.2 jit_solution(16865628334535550815)
XLA Ops:
  0.6 0.0 copy-start
  0.6 2.0 %shard_map.129 = f32[576,128]{1,0:T(8,128)} custom-call(f32[128,256]{1,0:T(8,128)} %filt_hbm.1, f32[128,256]{1,0:T(8,128)} %cot_hbm.1, s32[1,128]{1,0:T(1,128)} %bitcast.16), custom_call_target="tpu_custom_call" | custom-call | tf_op jit(solution)/shard_map/pallas_call | solution.py:245
  2.6 0.0 copy-start.3
  2.6 14.9 %all-to-all-start = ((f32[64,1,1152]{2,1,0:T(1,128)}), f32[64,1,1152]{2,1,0:T(1,128)S(1)}, u32[]{:S(2)}, u32[]{:S(2)}) async-start(f32[64,1,1152]{2,1,0:T(1,128)} %bitcast.14), calls=%async_computation | async-start | bytes 589824 | tf_op jit(solution)/shard_map/all_to_all | solution.py:261
  17.6 0.0 copy-done
  17.6 0.0 copy-done.3
  17.6 0.0 copy-start.1
  17.6 0.0 copy-start.2
  17.6 0.0 copy-start.4
  17.6 0.0 copy-start.5
  17.6 0.0 copy-start.6
  17.6 0.5 shard_map.130
  18.1 0.1 collective-permute-start
  18.2 1.1 %collective-permute-start.1 = (f32[48,128]{1,0:T(8,128)S(1)}, f32[48,128]{1,0:T(8,128)S(1)}, u32[]{:S(2)}, u32[]{:S(2)}) collective-permute-start(f32[48,128]{1,0:T(8,128)S(1)} %get-tuple-element.15), channel_id=1, source_target_pairs={{0,2},{1,3},{2,0},{3,1},{4,6},{5,7},{6,4},{7,5},{8,10},{9,11},{10,... | collective-permute-start | bytes 73736 | tf_op jit(solution)/shard_map/ppermute | solution.py:299
  19.3 0.8 %collective-permute-start.2 = (f32[48,128]{1,0:T(8,128)S(1)}, f32[48,128]{1,0:T(8,128)S(1)}, u32[]{:S(2)}, u32[]{:S(2)}) collective-permute-start(f32[48,128]{1,0:T(8,128)S(1)} %get-tuple-element.16), channel_id=1, source_target_pairs={{0,3},{1,2},{2,1},{3,0},{4,7},{5,6},{6,5},{7,4},{8,11},{9,10},{10,... | collective-permute-start | bytes 73736 | tf_op jit(solution)/shard_map/ppermute | solution.py:299
  20.1 0.0 collective-permute-done.part_1
  20.1 5.1 %collective-permute-done.1.part_2 = f32[48,128]{1,0:T(8,128)S(1)} collective-permute-done((f32[48,128]{1,0:T(8,128)S(1)}, f32[48,128]{1,0:T(8,128)S(1)}, u32[]{:S(2)}, u32[]{:S(2)}) %collective-permute-start.1) | collective-permute-done | bytes 24608 | tf_op jit(solution)/shard_map/ppermute | solution.py:299
  25.2 0.0 collective-permute-done.2.part_3
  25.2 4.0 %all-to-all-done = f32[64,1,1152]{2,1,0:T(1,128)S(1)} async-done(((f32[64,1,1152]{2,1,0:T(1,128)}), f32[64,1,1152]{2,1,0:T(1,128)S(1)}, u32[]{:S(2)}, u32[]{:S(2)}) %all-to-all-start) | async-done | bytes 294944 | tf_op jit(solution)/shard_map/all_to_all | solution.py:261
  29.2 0.0 copy-done.1
  29.2 0.0 copy-done.2
  29.2 0.0 copy-done.4
  29.2 0.0 copy-done.5
  29.2 0.0 copy-done.6
  29.2 3.3 %shard_map.131 = (f32[1280,128]{1,0:T(8,128)}, f32[1024,128]{1,0:T(8,128)S(1)}) custom-call(f32[576,128]{1,0:T(8,128)S(1)} %bitcast.9, f32[48,128]{1,0:T(8,128)S(1)} %get-tuple-element.13.part_0, f32[48,128]{1,0:T(8,128)S(1)} %collective-permute-done.part_1, f32[48,128]{1,0:T(8,128)S(1)} %collective-permute-done.1.part_2, ...), custom_call_target="tpu_custom_call" | custom-call | tf_op jit(solution)/shard_map/pallas_call | solution.py:245
  32.5 9.0 %all-to-all-start.1 = ((f32[64,1,2560]{2,1,0:T(1,128)}), f32[64,1,2560]{2,1,0:T(1,128)S(1)}, u32[]{:S(2)}, u32[]{:S(2)}) async-start(f32[64,1,2560]{2,1,0:T(1,128)} %bitcast.4), calls=%async_computation.1 | async-start | bytes 1310720 | tf_op jit(solution)/shard_map/all_to_all | solution.py:261
  41.5 0.9 %shard_map.133 = f32[64,128]{1,0:T(8,128)S(1)} custom-call(f32[576,128]{1,0:T(8,128)S(1)} %bitcast.10, f32[1024,128]{1,0:T(8,128)S(1)} %get-tuple-element.21.grads_ref), custom_call_target="tpu_custom_call" | custom-call | tf_op jit(solution)/shard_map/pallas_call | solution.py:245
  42.4 10.0 %all-gather = f32[256,128]{1,0:T(8,128)S(1)} all-gather(f32[64,128]{1,0:T(8,128)S(1)} %shard_map.133), channel_id=2, replica_groups=mesh['seq'=64,'red'=4] {'red'}, dimensions={0}, use_global_device_ids=true | all-gather | bytes 163840 | tf_op jit(solution)/shard_map/all_gather | solution.py:318
  52.4 1.0 %shard_map.134 = f32[3,4,4,1024]{3,2,1,0:T(4,128)} custom-call(f32[4,64,128]{2,1,0:T(8,128)S(1)} %bitcast.12, bf16[512,1024]{1,0:T(8,128)(2,1)S(1)} %copy-done), custom_call_target="tpu_custom_call" | custom-call | tf_op jit(solution)/shard_map/pallas_call | solution.py:245
  53.4 7.9 %all-to-all-done.1 = f32[64,1,2560]{2,1,0:T(1,128)S(1)} async-done(((f32[64,1,2560]{2,1,0:T(1,128)}), f32[64,1,2560]{2,1,0:T(1,128)S(1)}, u32[]{:S(2)}, u32[]{:S(2)}) %all-to-all-start.1) | async-done | bytes 655392 | tf_op jit(solution)/shard_map/all_to_all | solution.py:261
  61.3 0.9 %shard_map.132 = (f32[128,256]{1,0:T(8,128)}, f32[128,256]{1,0:T(8,128)}, bf16[3,128,256]{2,1,0:T(8,128)(2,1)}) custom-call(f32[1280,128]{1,0:T(8,128)S(1)} %bitcast.11), custom_call_target="tpu_custom_call" | custom-call | tf_op jit(solution)/shard_map/pallas_call | solution.py:245
Async XLA Ops:
  0.6 16.9 %copy-start = (bf16[512,1024]{1,0:T(8,128)(2,1)S(1)}, bf16[512,1024]{1,0:T(8,128)(2,1)}, u32[]{:S(2)}) copy-start(bf16[512,1024]{1,0:T(8,128)(2,1)} %emb_ref.3) | copy-start | bytes 3145732
  2.6 15.0 %copy-start.3 = (bf16[1024,3,4,4]{0,3,2,1:T(4,128)(2,1)S(1)}, bf16[1024,3,4,4]{0,3,2,1:T(4,128)(2,1)}, u32[]{:S(2)}) copy-start(bf16[1024,3,4,4]{0,3,2,1:T(4,128)(2,1)} %param.12) | copy-start | bytes 294916
  2.6 26.6 %all-to-all-start = ((f32[64,1,1152]{2,1,0:T(1,128)}), f32[64,1,1152]{2,1,0:T(1,128)S(1)}, u32[]{:S(2)}, u32[]{:S(2)}) async-start(f32[64,1,1152]{2,1,0:T(1,128)} %bitcast.14), calls=%async_computation | async-start | bytes 589824 | tf_op jit(solution)/shard_map/all_to_all | solution.py:261
  17.6 11.6 %copy-start.1 = (bf16[2,256,256]{2,1,0:T(8,128)(2,1)S(1)}, bf16[2,256,256]{2,1,0:T(8,128)(2,1)}, u32[]{:S(2)}) copy-start(bf16[2,256,256]{2,1,0:T(8,128)(2,1)} %constant.14.clone.backward_ref) | copy-start | bytes 786436
  17.6 11.6 %copy-start.2 = (bf16[2,256,256]{2,1,0:T(8,128)(2,1)S(1)}, bf16[2,256,256]{2,1,0:T(8,128)(2,1)}, u32[]{:S(2)}) copy-start(bf16[2,256,256]{2,1,0:T(8,128)(2,1)} %constant.13.clone.forward_ref) | copy-start | bytes 786436
  17.6 11.6 %copy-start.4 = (f32[2,64,128]{2,1,0:T(8,128)S(1)}, f32[2,64,128]{2,1,0:T(8,128)}, u32[]{:S(2)}) copy-start(f32[2,64,128]{2,1,0:T(8,128)} %constant.12.clone.twiddle_ref) | copy-start | bytes 196612
  17.6 11.6 %copy-start.5 = (bf16[128,192]{1,0:T(8,128)(2,1)S(1)}, bf16[128,192]{1,0:T(8,128)(2,1)}, u32[]{:S(2)}) copy-start(bf16[128,192]{1,0:T(8,128)(2,1)} %constant.10.clone.first_ref) | copy-start | bytes 147460
  17.6 11.6 %copy-start.6 = (bf16[64,384]{1,0:T(8,128)(2,1)S(1)}, bf16[64,384]{1,0:T(8,128)(2,1)}, u32[]{:S(2)}) copy-start(bf16[64,384]{1,0:T(8,128)(2,1)} %constant.11.clone.last_ref) | copy-start | bytes 147460
  18.1 2.0 %collective-permute-start = (f32[48,128]{1,0:T(8,128)S(1)}, f32[48,128]{1,0:T(8,128)S(1)}, u32[]{:S(2)}, u32[]{:S(2)}) collective-permute-start(f32[48,128]{1,0:T(8,128)S(1)} %get-tuple-element.14), channel_id=1, source_target_pairs={{0,1},{1,0},{2,3},{3,2},{4,5},{5,4},{6,7},{7,6},{8,9},{9,8},{10,11... | collective-permute-start | bytes 73736 | tf_op jit(solution)/shard_map/ppermute | solution.py:299
  18.2 6.9 %collective-permute-start.1 = (f32[48,128]{1,0:T(8,128)S(1)}, f32[48,128]{1,0:T(8,128)S(1)}, u32[]{:S(2)}, u32[]{:S(2)}) collective-permute-start(f32[48,128]{1,0:T(8,128)S(1)} %get-tuple-element.15), channel_id=1, source_target_pairs={{0,2},{1,3},{2,0},{3,1},{4,6},{5,7},{6,4},{7,5},{8,10},{9,11},{10,... | collective-permute-start | bytes 73736 | tf_op jit(solution)/shard_map/ppermute | solution.py:299
  19.3 5.8 %collective-permute-start.2 = (f32[48,128]{1,0:T(8,128)S(1)}, f32[48,128]{1,0:T(8,128)S(1)}, u32[]{:S(2)}, u32[]{:S(2)}) collective-permute-start(f32[48,128]{1,0:T(8,128)S(1)} %get-tuple-element.16), channel_id=1, source_target_pairs={{0,3},{1,2},{2,1},{3,0},{4,7},{5,6},{6,5},{7,4},{8,11},{9,10},{10,... | collective-permute-start | bytes 73736 | tf_op jit(solution)/shard_map/ppermute | solution.py:299
  32.5 28.7 %all-to-all-start.1 = ((f32[64,1,2560]{2,1,0:T(1,128)}), f32[64,1,2560]{2,1,0:T(1,128)S(1)}, u32[]{:S(2)}, u32[]{:S(2)}) async-start(f32[64,1,2560]{2,1,0:T(1,128)} %bitcast.4), calls=%async_computation.1 | async-start | bytes 1310720 | tf_op jit(solution)/shard_map/all_to_all | solution.py:261

commit v5 on v4

--- a/solution.py
+++ b/solution.py
@@ -12,6 +12,7 @@
 
 
 BLOCKS = 64
+PLANE = 16
 LANES = 128
 OWN = 4
 IN_ROWS = 9
@@ -63,6 +64,10 @@
         in_ref[pl.ds(place * IN_ROWS + row, BLOCKS // 2, stride=IN_ROWS), :] for place in (BLOCKS // 2, 0)
     ]
     return jnp.concatenate(halves, axis=0)
+
+
+def planes_reversed(value):
+    return jnp.concatenate([value[at : at + PLANE] for at in range(BLOCKS - PLANE, -1, -PLANE)], axis=0)
 
 
 def pack_kernel(filt_hbm, cot_hbm, ids_hbm, out_ref, filt, cot, ids, turn_ref, sems):
@@ -180,7 +185,7 @@
         grads = (cotangent[c] * conv, grad_inner * values[c], grad_inner * keys[c])
         sent = (*grads, queries[c] * conv, filter_grad * scale)
         for number, value in enumerate(sent):
-            out_ref[pl.ds(number * OWN + c, BLOCKS, stride=OUT_ROWS), :] = value
+            out_ref[pl.ds(number * OWN + c, BLOCKS, stride=OUT_ROWS), :] = planes_reversed(value)
         for number, value in enumerate(grads):
             grads_ref[pl.ds(number * OWN + c, BLOCKS, stride=16), :] = value
 
@@ -228,9 +233,9 @@
 def unpack_kernel(in_ref, output_ref, filter_ref, branch_ref, turn_ref):
     for number in range(OUT_ROWS // OWN):
         for c in range(OWN):
-            turn_ref[number, pl.ds(c, BLOCKS, stride=OWN), :] = in_ref[
-                pl.ds(number * OWN + c, BLOCKS, stride=OUT_ROWS), :
-            ]
+            turn_ref[number, pl.ds(c, BLOCKS, stride=OWN), :] = planes_reversed(
+                in_ref[pl.ds(number * OWN + c, BLOCKS, stride=OUT_ROWS), :]
+            )
         value = turn_ref[number].T
         if number < 3:
             branch_ref[number] = value.astype(BF16)
@@ -255,10 +260,9 @@
     return jax.ShapeDtypeStruct(dims, dtype)
 
 
-def exchange(value, axis, pieces, rows, first=0):
-    order = [(first + place) % pieces for place in range(pieces)]
+def exchange(value, axis, pieces, rows, order):
     sent = value.reshape(pieces, 1, rows * LANES)
-    got = lax.all_to_all(sent, axis, split_axis=0, concat_axis=0, tiled=True, axis_index_groups=[order])
+    got = lax.all_to_all(sent, axis, split_axis=0, concat_axis=0, tiled=True, axis_index_groups=[list(order)])
     return got.reshape(pieces * rows, LANES)
 
 
@@ -270,6 +274,7 @@
     groups = vocabulary // LANES
     positions, channels = filters.shape
     scale = float(positions * blocks) ** (-0.5)
+    numbers = np.arange(BLOCKS)
 
     packed = call(
         pack_kernel,
@@ -287,7 +292,7 @@
         space=pl.ANY,
         limit=60 * 2**20,
     )
-    arrived = exchange(packed, "seq", BLOCKS, IN_ROWS, first=BLOCKS // 2)
+    arrived = exchange(packed, "seq", BLOCKS, IN_ROWS, np.roll(numbers, BLOCKS // 2).tolist())
     parts = call(
         table_kernel,
         [shape((groups * branches * piece, LANES))] * reds,
@@ -307,7 +312,7 @@
         *parts,
         *constants,
     )
-    returned = exchange(results, "seq", BLOCKS, OUT_ROWS)
+    returned = exchange(results, "seq", BLOCKS, OUT_ROWS, numbers.reshape(-1, PLANE)[::-1].ravel().tolist())
     sums = call(
         sums_kernel,
         shape((groups * 16, LANES)),

time: 62.5 us -> 62 us (level)
  waiting for transfers between devices: 17 us -> 12.3 us
  blocking collectives: 9.99 us -> 13.8 us
    all_to_all x2, waiting for transfers between devices: 11.9 us -> 7.27 us  [exchange(): lax.all_to_all(sent, axis, split_axis=0, concat_axis=0, tiled=True, axis_...]
    all_gather x1, blocking collectives: 9.99 us -> 13.8 us  [shards(): gathered = lax.all_gather(sums, 'red', axis=0)]
where the time goes in v5:
time: 62 us; the launch traced here: 61.7 us
  starting transfers between devices  26.2 us (42%)
  blocking collectives  13.8 us (22%)
  waiting for transfers between devices  12.3 us (20%)
  Pallas kernels  8.55 us (14%)
  between operations  0.78 us (1%)
    all_to_all x2, starting transfers between devices, exchange(): lax.all_to_all(sent, axis, split_axis=0, concat_axis=0, tiled=True, axis_...  24.2 us
    all_gather x1, blocking collectives, shards(): gathered = lax.all_gather(sums, 'red', axis=0)  13.8 us
    pallas_call x6, Pallas kernels, call(): pl.pallas_call(body, in_specs=[pl.BlockSpec(memory_space=space)] * len(op...  8.55 us
    all_to_all x2, waiting for transfers between devices, exchange(): lax.all_to_all(sent, axis, split_axis=0, concat_axis=0, tiled=True, axis_...  7.27 us
    ppermute x3, waiting for transfers between devices, shards(): lax.ppermute(parts[apart], 'red', [(q, q ^ apart) for q in range(reds)])  5.07 us
    ppermute x3, starting transfers between devices, shards(): lax.ppermute(parts[apart], 'red', [(q, q ^ apart) for q in range(reds)])  1.96 us
  transfers between devices with their start and end apart: 5, of which 3 were waited for; matrix products, arithmetic and copies ran while one was open for 0% of the time, Pallas kernels for 4%

profile of v5, /device:TPU:32, one launch (start us, length us, event | category | flops | bytes accessed | tf_op | source)
XLA Modules:
  0.0 61.7 jit_solution(9670644586152575448)
XLA Ops:
  0.6 0.0 copy-start
  0.6 2.0 %shard_map.129 = f32[576,128]{1,0:T(8,128)} custom-call(f32[128,256]{1,0:T(8,128)} %filt_hbm.1, f32[128,256]{1,0:T(8,128)} %cot_hbm.1, s32[1,128]{1,0:T(1,128)} %bitcast.16), custom_call_target="tpu_custom_call" | custom-call | tf_op jit(solution)/shard_map/pallas_call | solution.py:250
  2.6 0.0 copy-start.3
  2.6 14.9 %all-to-all-start = ((f32[64,1,1152]{2,1,0:T(1,128)}), f32[64,1,1152]{2,1,0:T(1,128)S(1)}, u32[]{:S(2)}, u32[]{:S(2)}) async-start(f32[64,1,1152]{2,1,0:T(1,128)} %bitcast.14), calls=%async_computation | async-start | bytes 589824 | tf_op jit(solution)/shard_map/all_to_all | solution.py:265
  17.6 0.0 copy-done
  17.6 0.0 copy-done.3
  17.6 0.0 copy-start.1
  17.6 0.0 copy-start.2
  17.6 0.0 copy-start.4
  17.6 0.0 copy-start.5
  17.6 0.0 copy-start.6
  17.6 0.5 shard_map.130
  18.1 0.1 collective-permute-start
  18.2 1.1 %collective-permute-start.1 = (f32[48,128]{1,0:T(8,128)S(1)}, f32[48,128]{1,0:T(8,128)S(1)}, u32[]{:S(2)}, u32[]{:S(2)}) collective-permute-start(f32[48,128]{1,0:T(8,128)S(1)} %get-tuple-element.15), channel_id=1, source_target_pairs={{0,2},{1,3},{2,0},{3,1},{4,6},{5,7},{6,4},{7,5},{8,10},{9,11},{10,... | collective-permute-start | bytes 73736 | tf_op jit(solution)/shard_map/ppermute | solution.py:304
  19.3 0.8 %collective-permute-start.2 = (f32[48,128]{1,0:T(8,128)S(1)}, f32[48,128]{1,0:T(8,128)S(1)}, u32[]{:S(2)}, u32[]{:S(2)}) collective-permute-start(f32[48,128]{1,0:T(8,128)S(1)} %get-tuple-element.16), channel_id=1, source_target_pairs={{0,3},{1,2},{2,1},{3,0},{4,7},{5,6},{6,5},{7,4},{8,11},{9,10},{10,... | collective-permute-start | bytes 73736 | tf_op jit(solution)/shard_map/ppermute | solution.py:304
  20.1 0.0 collective-permute-done.part_1
  20.1 5.1 %collective-permute-done.1.part_2 = f32[48,128]{1,0:T(8,128)S(1)} collective-permute-done((f32[48,128]{1,0:T(8,128)S(1)}, f32[48,128]{1,0:T(8,128)S(1)}, u32[]{:S(2)}, u32[]{:S(2)}) %collective-permute-start.1) | collective-permute-done | bytes 24608 | tf_op jit(solution)/shard_map/ppermute | solution.py:304
  25.2 0.0 collective-permute-done.2.part_3
  25.2 4.0 %all-to-all-done = f32[64,1,1152]{2,1,0:T(1,128)S(1)} async-done(((f32[64,1,1152]{2,1,0:T(1,128)}), f32[64,1,1152]{2,1,0:T(1,128)S(1)}, u32[]{:S(2)}, u32[]{:S(2)}) %all-to-all-start) | async-done | bytes 294944 | tf_op jit(solution)/shard_map/all_to_all | solution.py:265
  29.2 0.0 copy-done.1
  29.2 0.0 copy-done.2
  29.2 0.0 copy-done.4
  29.2 0.0 copy-done.5
  29.2 0.0 copy-done.6
  29.2 3.3 %shard_map.131 = (f32[1280,128]{1,0:T(8,128)}, f32[1024,128]{1,0:T(8,128)S(1)}) custom-call(f32[576,128]{1,0:T(8,128)S(1)} %bitcast.9, f32[48,128]{1,0:T(8,128)S(1)} %get-tuple-element.13.part_0, f32[48,128]{1,0:T(8,128)S(1)} %collective-permute-done.part_1, f32[48,128]{1,0:T(8,128)S(1)} %collective-permute-done.1.part_2, ...), custom_call_target="tpu_custom_call" | custom-call | tf_op jit(solution)/shard_map/pallas_call | solution.py:250
  32.5 9.3 %all-to-all-start.1 = ((f32[64,1,2560]{2,1,0:T(1,128)}), f32[64,1,2560]{2,1,0:T(1,128)S(1)}, u32[]{:S(2)}, u32[]{:S(2)}) async-start(f32[64,1,2560]{2,1,0:T(1,128)} %bitcast.4), calls=%async_computation.1 | async-start | bytes 1310720 | tf_op jit(solution)/shard_map/all_to_all | solution.py:265
  41.8 0.8 %shard_map.133 = f32[64,128]{1,0:T(8,128)S(1)} custom-call(f32[576,128]{1,0:T(8,128)S(1)} %bitcast.10, f32[1024,128]{1,0:T(8,128)S(1)} %get-tuple-element.21.grads_ref), custom_call_target="tpu_custom_call" | custom-call | tf_op jit(solution)/shard_map/pallas_call | solution.py:250
  42.7 13.8 %all-gather = f32[256,128]{1,0:T(8,128)S(1)} all-gather(f32[64,128]{1,0:T(8,128)S(1)} %shard_map.133), channel_id=2, replica_groups=mesh['seq'=64,'red'=4] {'red'}, dimensions={0}, use_global_device_ids=true | all-gather | bytes 163840 | tf_op jit(solution)/shard_map/all_gather | solution.py:323
  56.4 1.0 %shard_map.134 = f32[3,4,4,1024]{3,2,1,0:T(4,128)} custom-call(f32[4,64,128]{2,1,0:T(8,128)S(1)} %bitcast.12, bf16[512,1024]{1,0:T(8,128)(2,1)S(1)} %copy-done), custom_call_target="tpu_custom_call" | custom-call | tf_op jit(solution)/shard_map/pallas_call | solution.py:250
  57.4 3.3 %all-to-all-done.1 = f32[64,1,2560]{2,1,0:T(1,128)S(1)} async-done(((f32[64,1,2560]{2,1,0:T(1,128)}), f32[64,1,2560]{2,1,0:T(1,128)S(1)}, u32[]{:S(2)}, u32[]{:S(2)}) %all-to-all-start.1) | async-done | bytes 655392 | tf_op jit(solution)/shard_map/all_to_all | solution.py:265
  60.7 0.9 %shard_map.132 = (f32[128,256]{1,0:T(8,128)}, f32[128,256]{1,0:T(8,128)}, bf16[3,128,256]{2,1,0:T(8,128)(2,1)}) custom-call(f32[1280,128]{1,0:T(8,128)S(1)} %bitcast.11), custom_call_target="tpu_custom_call" | custom-call | tf_op jit(solution)/shard_map/pallas_call | solution.py:250
Async XLA Ops:
  0.6 16.9 %copy-start = (bf16[512,1024]{1,0:T(8,128)(2,1)S(1)}, bf16[512,1024]{1,0:T(8,128)(2,1)}, u32[]{:S(2)}) copy-start(bf16[512,1024]{1,0:T(8,128)(2,1)} %emb_ref.3) | copy-start | bytes 3145732
  2.6 15.0 %copy-start.3 = (bf16[1024,3,4,4]{0,3,2,1:T(4,128)(2,1)S(1)}, bf16[1024,3,4,4]{0,3,2,1:T(4,128)(2,1)}, u32[]{:S(2)}) copy-start(bf16[1024,3,4,4]{0,3,2,1:T(4,128)(2,1)} %param.12) | copy-start | bytes 294916
  2.6 26.6 %all-to-all-start = ((f32[64,1,1152]{2,1,0:T(1,128)}), f32[64,1,1152]{2,1,0:T(1,128)S(1)}, u32[]{:S(2)}, u32[]{:S(2)}) async-start(f32[64,1,1152]{2,1,0:T(1,128)} %bitcast.14), calls=%async_computation | async-start | bytes 589824 | tf_op jit(solution)/shard_map/all_to_all | solution.py:265
  17.6 11.6 %copy-start.1 = (bf16[2,256,256]{2,1,0:T(8,128)(2,1)S(1)}, bf16[2,256,256]{2,1,0:T(8,128)(2,1)}, u32[]{:S(2)}) copy-start(bf16[2,256,256]{2,1,0:T(8,128)(2,1)} %constant.14.clone.backward_ref) | copy-start | bytes 786436
  17.6 11.6 %copy-start.2 = (bf16[2,256,256]{2,1,0:T(8,128)(2,1)S(1)}, bf16[2,256,256]{2,1,0:T(8,128)(2,1)}, u32[]{:S(2)}) copy-start(bf16[2,256,256]{2,1,0:T(8,128)(2,1)} %constant.13.clone.forward_ref) | copy-start | bytes 786436
  17.6 11.6 %copy-start.4 = (f32[2,64,128]{2,1,0:T(8,128)S(1)}, f32[2,64,128]{2,1,0:T(8,128)}, u32[]{:S(2)}) copy-start(f32[2,64,128]{2,1,0:T(8,128)} %constant.12.clone.twiddle_ref) | copy-start | bytes 196612
  17.6 11.6 %copy-start.5 = (bf16[128,192]{1,0:T(8,128)(2,1)S(1)}, bf16[128,192]{1,0:T(8,128)(2,1)}, u32[]{:S(2)}) copy-start(bf16[128,192]{1,0:T(8,128)(2,1)} %constant.10.clone.first_ref) | copy-start | bytes 147460
  17.6 11.6 %copy-start.6 = (bf16[64,384]{1,0:T(8,128)(2,1)S(1)}, bf16[64,384]{1,0:T(8,128)(2,1)}, u32[]{:S(2)}) copy-start(bf16[64,384]{1,0:T(8,128)(2,1)} %constant.11.clone.last_ref) | copy-start | bytes 147460
  18.1 2.0 %collective-permute-start = (f32[48,128]{1,0:T(8,128)S(1)}, f32[48,128]{1,0:T(8,128)S(1)}, u32[]{:S(2)}, u32[]{:S(2)}) collective-permute-start(f32[48,128]{1,0:T(8,128)S(1)} %get-tuple-element.14), channel_id=1, source_target_pairs={{0,1},{1,0},{2,3},{3,2},{4,5},{5,4},{6,7},{7,6},{8,9},{9,8},{10,11... | collective-permute-start | bytes 73736 | tf_op jit(solution)/shard_map/ppermute | solution.py:304
  18.2 6.9 %collective-permute-start.1 = (f32[48,128]{1,0:T(8,128)S(1)}, f32[48,128]{1,0:T(8,128)S(1)}, u32[]{:S(2)}, u32[]{:S(2)}) collective-permute-start(f32[48,128]{1,0:T(8,128)S(1)} %get-tuple-element.15), channel_id=1, source_target_pairs={{0,2},{1,3},{2,0},{3,1},{4,6},{5,7},{6,4},{7,5},{8,10},{9,11},{10,... | collective-permute-start | bytes 73736 | tf_op jit(solution)/shard_map/ppermute | solution.py:304
  19.3 5.8 %collective-permute-start.2 = (f32[48,128]{1,0:T(8,128)S(1)}, f32[48,128]{1,0:T(8,128)S(1)}, u32[]{:S(2)}, u32[]{:S(2)}) collective-permute-start(f32[48,128]{1,0:T(8,128)S(1)} %get-tuple-element.16), channel_id=1, source_target_pairs={{0,3},{1,2},{2,1},{3,0},{4,7},{5,6},{6,5},{7,4},{8,11},{9,10},{10,... | collective-permute-start | bytes 73736 | tf_op jit(solution)/shard_map/ppermute | solution.py:304
  32.5 28.2 %all-to-all-start.1 = ((f32[64,1,2560]{2,1,0:T(1,128)}), f32[64,1,2560]{2,1,0:T(1,128)S(1)}, u32[]{:S(2)}, u32[]{:S(2)}) async-start(f32[64,1,2560]{2,1,0:T(1,128)} %bitcast.4), calls=%async_computation.1 | async-start | bytes 1310720 | tf_op jit(solution)/shard_map/all_to_all | solution.py:265

commit v6 on v5

--- a/solution.py
+++ b/solution.py
@@ -100,10 +100,13 @@
             rows_ref[at : at + piece, :] = proj_ref[b, q].astype(F32)
     table_ref[...] = dot_last(rows_ref[...].astype(BF16), emb_ref[...])
     place = lax.axis_index("red")
-    for apart, out_ref in enumerate(out_refs):
+    own_ref, pair_ref, across_ref = out_refs
+    held = across_ref.shape[0]
+    for apart, out_ref, base in ((0, own_ref, 0), (1, pair_ref, 0), (3, pair_ref, held), (2, across_ref, 0)):
         rows = table_ref[pl.ds(pl.multiple_of((place ^ apart) * 16, 16), 16), :]
         for part in range(rows.shape[1] // LANES):
-            out_ref[part * wide : (part + 1) * wide, :] = rows[:wide, part * LANES : (part + 1) * LANES]
+            at = base + part * wide
+            out_ref[at : at + wide, :] = rows[:wide, part * LANES : (part + 1) * LANES]
 
 
 def right_product(value, matrix_ref):
@@ -114,7 +117,7 @@
 
 
 def conv_kernel(
-    scale, in_ref, part_0, part_1, part_2, part_3, first_ref, last_ref, twiddle_ref, forward_ref, backward_ref, out_ref, grads_ref
+    scale, in_ref, part_0, part_1, part_2, first_ref, last_ref, twiddle_ref, forward_ref, backward_ref, out_ref, grads_ref
 ):
     wide = 3 * OWN
     groups = part_0.shape[0] // wide
@@ -122,7 +125,7 @@
     def received(row):
         return in_blocks_order(in_ref, row)
 
-    table = (part_0[...] + part_1[...]) + (part_2[...] + part_3[...])
+    table = (part_0[...] + part_1[: part_0.shape[0]]) + part_2[...]
     ids = received(2 * OWN).astype(jnp.int32)
     lane = ids & (LANES - 1)
     group = ids >> 7
@@ -293,16 +296,17 @@
         limit=60 * 2**20,
     )
     arrived = exchange(packed, "seq", BLOCKS, IN_ROWS, np.roll(numbers, BLOCKS // 2).tolist())
-    parts = call(
+    held = groups * branches * piece
+    own, pair, across = call(
         table_kernel,
-        [shape((groups * branches * piece, LANES))] * reds,
+        [shape((held, LANES)), shape((2 * held, LANES)), shape((held, LANES))],
         [pltpu.VMEM((reds * 16, width_rows), F32), pltpu.VMEM((reds * 16, vocabulary), F32)],
         proj_weight.transpose(1, 2, 3, 0),
         embedding,
     )
-    parts = [parts[0]] + [
-        lax.ppermute(parts[apart], "red", [(q, q ^ apart) for q in range(reds)]) for apart in range(1, reds)
-    ]
+    pair = lax.ppermute(pair, "red", [(q, q ^ 1) for q in range(reds)])
+    across = lax.ppermute(across + pair[held:], "red", [(q, q ^ 2) for q in range(reds)])
+    parts = [own, pair, across]
     constants = [jnp.asarray(c) for c in transform_constants()]
     results, grads = call(
         functools.partial(conv_kernel, scale),

time: 62 us -> 62 us (level); the launches traced: 61.7 us -> 61 us
  blocking collectives: 13.8 us -> 12.2 us
  waiting for transfers between devices: 12.3 us -> 13.8 us
    all_gather x1, blocking collectives: 13.8 us -> 12.2 us  [shards(): gathered = lax.all_gather(sums, 'red', axis=0)]
    ppermute x3 -> x2, starting transfers between devices: 1.96 us -> 1.1 us  [the longest x1 1.01 us: shards(): lax.ppermute(across + pair[held:], 'red', [(q, q ^ 2) for q in range(reds)])]
    all_to_all x2, waiting for transfers between devices: 7.27 us -> 8.12 us  [exchange(): lax.all_to_all(sent, axis, split_axis=0, concat_axis=0, tiled=True, axis_...]
    ppermute x3 -> x2, waiting for transfers between devices: 5.07 us -> 5.66 us  [the longest x1 4.44 us: shards(): lax.ppermute(across + pair[held:], 'red', [(q, q ^ 2) for q in range(reds)])]
  transfers between devices with their start and end apart: 5 -> 4, of which waited for: 3 -> 4; matrix products, arithmetic and copies ran while one was open for 0% -> 0% of each run, Pallas kernels for 4% -> 4%
where the time goes in v6:
time: 62 us; the launch traced here: 61 us
  starting transfers between devices  25.7 us (41%)
  waiting for transfers between devices  13.8 us (22%)
  blocking collectives  12.2 us (20%)
  Pallas kernels  8.54 us (14%)
  between operations  0.78 us (1%)
    all_to_all x2, starting transfers between devices, exchange(): lax.all_to_all(sent, axis, split_axis=0, concat_axis=0, tiled=True, axis_...  24.6 us
    all_gather x1, blocking collectives, shards(): gathered = lax.all_gather(sums, 'red', axis=0)  12.2 us
    pallas_call x6, Pallas kernels, call(): pl.pallas_call(body, in_specs=[pl.BlockSpec(memory_space=space)] * len(op...  8.54 us
    all_to_all x2, waiting for transfers between devices, exchange(): lax.all_to_all(sent, axis, split_axis=0, concat_axis=0, tiled=True, axis_...  8.12 us
    ppermute x1, waiting for transfers between devices, shards(): lax.ppermute(across + pair[held:], 'red', [(q, q ^ 2) for q in range(reds)])  4.44 us
  transfers between devices with their start and end apart: 4, of which 4 were waited for; matrix products, arithmetic and copies ran while one was open for 0% of the time, Pallas kernels for 4%

profile of v6, /device:TPU:32, one launch (start us, length us, event | category | flops | bytes accessed | tf_op | source)
XLA Modules:
  0.0 61.0 jit_solution(7189919893878534900)
XLA Ops:
  0.6 0.0 copy-start
  0.6 1.9 %shard_map.129 = f32[576,128]{1,0:T(8,128)} custom-call(f32[128,256]{1,0:T(8,128)} %filt_hbm.1, f32[128,256]{1,0:T(8,128)} %cot_hbm.1, s32[1,128]{1,0:T(1,128)} %bitcast.16), custom_call_target="tpu_custom_call" | custom-call | tf_op jit(solution)/shard_map/pallas_call | solution.py:253
  2.6 0.0 copy-start.3
  2.6 14.9 %all-to-all-start = ((f32[64,1,1152]{2,1,0:T(1,128)}), f32[64,1,1152]{2,1,0:T(1,128)S(1)}, u32[]{:S(2)}, u32[]{:S(2)}) async-start(f32[64,1,1152]{2,1,0:T(1,128)} %bitcast.14), calls=%async_computation | async-start | bytes 589824 | tf_op jit(solution)/shard_map/all_to_all | solution.py:268
  17.5 0.0 copy-done
  17.6 0.0 copy-done.3
  17.6 0.0 copy-start.1
  17.6 0.0 copy-start.2
  17.6 0.0 copy-start.5
  17.6 0.0 copy-start.6
  17.6 0.5 shard_map.130
  18.1 0.0 copy-start.4
  18.1 0.1 collective-permute-start
  18.2 1.2 %collective-permute-done.part_1 = f32[96,128]{1,0:T(8,128)S(1)} collective-permute-done((f32[96,128]{1,0:T(8,128)S(1)}, f32[96,128]{1,0:T(8,128)S(1)}, u32[]{:S(2)}, u32[]{:S(2)}) %collective-permute-start) | collective-permute-done | bytes 49184 | tf_op jit(solution)/shard_map/ppermute | solution.py:307
  19.4 1.0 %collective-permute-start.1 = (f32[48,128]{1,0:T(8,128)S(1)}, f32[48,128]{1,0:T(8,128)S(1)}, u32[]{:S(2)}, u32[]{:S(2)}) collective-permute-start(f32[48,128]{1,0:T(8,128)S(1)} %slice_add_fusion), channel_id=1, source_target_pairs={{0,2},{1,3},{2,0},{3,1},{4,6},{5,7},{6,4},{7,5},{8,10},{9,11},{10,... | collective-permute-start | bytes 73736 | tf_op jit(solution)/shard_map/ppermute | solution.py:308
  20.4 4.4 %collective-permute-done.1.part_2 = f32[48,128]{1,0:T(8,128)S(1)} collective-permute-done((f32[48,128]{1,0:T(8,128)S(1)}, f32[48,128]{1,0:T(8,128)S(1)}, u32[]{:S(2)}, u32[]{:S(2)}) %collective-permute-start.1) | collective-permute-done | bytes 24608 | tf_op jit(solution)/shard_map/ppermute | solution.py:308
  24.9 3.6 %all-to-all-done = f32[64,1,1152]{2,1,0:T(1,128)S(1)} async-done(((f32[64,1,1152]{2,1,0:T(1,128)}), f32[64,1,1152]{2,1,0:T(1,128)S(1)}, u32[]{:S(2)}, u32[]{:S(2)}) %all-to-all-start) | async-done | bytes 294944 | tf_op jit(solution)/shard_map/all_to_all | solution.py:268
  28.5 0.0 copy-done.1
  28.5 0.0 copy-done.2
  28.5 0.0 copy-done.5
  28.5 0.0 copy-done.6
  28.5 0.0 copy-done.4
  28.6 3.3 %shard_map.131 = (f32[1280,128]{1,0:T(8,128)}, f32[1024,128]{1,0:T(8,128)S(1)}) custom-call(f32[576,128]{1,0:T(8,128)S(1)} %bitcast.9, f32[48,128]{1,0:T(8,128)S(1)} %get-tuple-element.12.part_0, f32[96,128]{1,0:T(8,128)S(1)} %collective-permute-done.part_1, f32[48,128]{1,0:T(8,128)S(1)} %collective-permute-done.1.part_2, bf16[128,192]{1,0:T(8,128)(2,1)S(1)} %copy-done.5, ...), custom_call_target="tpu_custom_call" | custom-call | tf_op jit(solution)/shard_map/pallas_call | solution.py:253
  31.9 9.7 %all-to-all-start.1 = ((f32[64,1,2560]{2,1,0:T(1,128)}), f32[64,1,2560]{2,1,0:T(1,128)S(1)}, u32[]{:S(2)}, u32[]{:S(2)}) async-start(f32[64,1,2560]{2,1,0:T(1,128)} %bitcast.4), calls=%async_computation.1 | async-start | bytes 1310720 | tf_op jit(solution)/shard_map/all_to_all | solution.py:268
  41.6 0.8 %shard_map.133 = f32[64,128]{1,0:T(8,128)S(1)} custom-call(f32[576,128]{1,0:T(8,128)S(1)} %bitcast.10, f32[1024,128]{1,0:T(8,128)S(1)} %get-tuple-element.19.grads_ref), custom_call_target="tpu_custom_call" | custom-call | tf_op jit(solution)/shard_map/pallas_call | solution.py:253
  42.4 12.2 %all-gather = f32[256,128]{1,0:T(8,128)S(1)} all-gather(f32[64,128]{1,0:T(8,128)S(1)} %shard_map.133), channel_id=2, replica_groups=mesh['seq'=64,'red'=4] {'red'}, dimensions={0}, use_global_device_ids=true | all-gather | bytes 163840 | tf_op jit(solution)/shard_map/all_gather | solution.py:327
  54.6 1.0 %shard_map.134 = f32[3,4,4,1024]{3,2,1,0:T(4,128)} custom-call(f32[4,64,128]{2,1,0:T(8,128)S(1)} %bitcast.12, bf16[512,1024]{1,0:T(8,128)(2,1)S(1)} %copy-done), custom_call_target="tpu_custom_call" | custom-call | tf_op jit(solution)/shard_map/pallas_call | solution.py:253
  55.6 4.5 %all-to-all-done.1 = f32[64,1,2560]{2,1,0:T(1,128)S(1)} async-done(((f32[64,1,2560]{2,1,0:T(1,128)}), f32[64,1,2560]{2,1,0:T(1,128)S(1)}, u32[]{:S(2)}, u32[]{:S(2)}) %all-to-all-start.1) | async-done | bytes 655392 | tf_op jit(solution)/shard_map/all_to_all | solution.py:268
  60.1 0.9 %shard_map.132 = (f32[128,256]{1,0:T(8,128)}, f32[128,256]{1,0:T(8,128)}, bf16[3,128,256]{2,1,0:T(8,128)(2,1)}) custom-call(f32[1280,128]{1,0:T(8,128)S(1)} %bitcast.11), custom_call_target="tpu_custom_call" | custom-call | tf_op jit(solution)/shard_map/pallas_call | solution.py:253
  (1 shorter events, 0.0 us)
Async XLA Ops:
  0.6 16.9 %copy-start = (bf16[512,1024]{1,0:T(8,128)(2,1)S(1)}, bf16[512,1024]{1,0:T(8,128)(2,1)}, u32[]{:S(2)}) copy-start(bf16[512,1024]{1,0:T(8,128)(2,1)} %emb_ref.3) | copy-start | bytes 3145732
  2.6 15.0 %copy-start.3 = (bf16[1024,3,4,4]{0,3,2,1:T(4,128)(2,1)S(1)}, bf16[1024,3,4,4]{0,3,2,1:T(4,128)(2,1)}, u32[]{:S(2)}) copy-start(bf16[1024,3,4,4]{0,3,2,1:T(4,128)(2,1)} %param.12) | copy-start | bytes 294916
  2.6 25.9 %all-to-all-start = ((f32[64,1,1152]{2,1,0:T(1,128)}), f32[64,1,1152]{2,1,0:T(1,128)S(1)}, u32[]{:S(2)}, u32[]{:S(2)}) async-start(f32[64,1,1152]{2,1,0:T(1,128)} %bitcast.14), calls=%async_computation | async-start | bytes 589824 | tf_op jit(solution)/shard_map/all_to_all | solution.py:268
  17.6 11.0 %copy-start.1 = (bf16[2,256,256]{2,1,0:T(8,128)(2,1)S(1)}, bf16[2,256,256]{2,1,0:T(8,128)(2,1)}, u32[]{:S(2)}) copy-start(bf16[2,256,256]{2,1,0:T(8,128)(2,1)} %constant.14.clone.backward_ref) | copy-start | bytes 786436
  17.6 11.0 %copy-start.2 = (bf16[2,256,256]{2,1,0:T(8,128)(2,1)S(1)}, bf16[2,256,256]{2,1,0:T(8,128)(2,1)}, u32[]{:S(2)}) copy-start(bf16[2,256,256]{2,1,0:T(8,128)(2,1)} %constant.13.clone.forward_ref) | copy-start | bytes 786436
  17.6 10.9 %copy-start.5 = (bf16[128,192]{1,0:T(8,128)(2,1)S(1)}, bf16[128,192]{1,0:T(8,128)(2,1)}, u32[]{:S(2)}) copy-start(bf16[128,192]{1,0:T(8,128)(2,1)} %constant.10.clone.first_ref) | copy-start | bytes 147460
  17.6 10.9 %copy-start.6 = (bf16[64,384]{1,0:T(8,128)(2,1)S(1)}, bf16[64,384]{1,0:T(8,128)(2,1)}, u32[]{:S(2)}) copy-start(bf16[64,384]{1,0:T(8,128)(2,1)} %constant.11.clone.last_ref) | copy-start | bytes 147460
  18.1 10.4 %copy-start.4 = (f32[2,64,128]{2,1,0:T(8,128)S(1)}, f32[2,64,128]{2,1,0:T(8,128)}, u32[]{:S(2)}) copy-start(f32[2,64,128]{2,1,0:T(8,128)} %constant.12.clone.twiddle_ref) | copy-start | bytes 196612
  18.1 1.3 %collective-permute-start = (f32[96,128]{1,0:T(8,128)S(1)}, f32[96,128]{1,0:T(8,128)S(1)}, u32[]{:S(2)}, u32[]{:S(2)}) collective-permute-start(f32[96,128]{1,0:T(8,128)S(1)} %get-tuple-element.13), channel_id=1, source_target_pairs={{0,1},{1,0},{2,3},{3,2},{4,5},{5,4},{6,7},{7,6},{8,9},{9,8},{10,11... | collective-permute-start | bytes 147464 | tf_op jit(solution)/shard_map/ppermute | solution.py:307
  19.4 5.4 %collective-permute-start.1 = (f32[48,128]{1,0:T(8,128)S(1)}, f32[48,128]{1,0:T(8,128)S(1)}, u32[]{:S(2)}, u32[]{:S(2)}) collective-permute-start(f32[48,128]{1,0:T(8,128)S(1)} %slice_add_fusion), channel_id=1, source_target_pairs={{0,2},{1,3},{2,0},{3,1},{4,6},{5,7},{6,4},{7,5},{8,10},{9,11},{10,... | collective-permute-start | bytes 73736 | tf_op jit(solution)/shard_map/ppermute | solution.py:308
  31.9 28.2 %all-to-all-start.1 = ((f32[64,1,2560]{2,1,0:T(1,128)}), f32[64,1,2560]{2,1,0:T(1,128)S(1)}, u32[]{:S(2)}, u32[]{:S(2)}) async-start(f32[64,1,2560]{2,1,0:T(1,128)} %bitcast.4), calls=%async_computation.1 | async-start | bytes 1310720 | tf_op jit(solution)/shard_map/all_to_all | solution.py:268
